TPU v7x, 32 devices: a whole 2x2x4 slice. The times are simulated.
32 devices in a mesh: groups: 2 (over y), fam: 4 (over z), trait: 2 (over x), rep: 2 (over core).
Axes of the slice: x: 2, y: 2, z: 4, core: 2. Of those that a mesh axis runs over, the one named last changes fastest.
Arguments:
- pheno: float32 [4096, 1024], P(('groups', 'fam'), 'trait'), parts along dimension 0, may hold values from -6 to 6
- match: int32 [4096], P(('groups', 'fam')), parts along dimension 0, may hold values from 0 to 2047, as said below
- diag_var: float32 [4096], P(('groups', 'fam')), parts along dimension 0, may hold values from 0.5 to 1.5
- tiles: float32 [256, 4096], P(('groups', 'fam', 'rep')), parts along dimension 0, may hold values from -0.375 to 0.375
- tile_row_family: int32 [256], P(('groups', 'fam', 'rep')), parts along dimension 0, may hold values from 0 to 7, as said below
- tile_cols: int32 [256], P(('groups', 'fam', 'rep')), parts along dimension 0, may hold values from 0 to 7
- rel_row: int32 [2048], P(('groups', 'fam', 'rep')), parts along dimension 0, may hold values from 0 to 511
- rel_peer: int32 [2048, 1], P(('groups', 'fam', 'rep')), parts along dimension 0, may hold values from 0 to 3; in each aligned block of 128 rows (0 to 127, 128 to 255, ...) at most 64 rows name the same one
- rel_slot: int32 [2048], P(('groups', 'fam', 'rep')), parts along dimension 0, may hold values from 0 to 511
- rel_weight: float32 [2048], P(('groups', 'fam', 'rep')), parts along dimension 0, may hold values from -4 to 4
Outputs:
- solution_field: float32 [4096, 1024], P(('groups', 'fam'), 'trait'), parts along dimension 0
- residual: float32 [4096, 1024], P(('groups', 'fam'), 'trait'), parts along dimension 0
There are 2 independent parts, one for each index of `groups`. A program takes and returns all parts, laid end to end along the dimension named above; each array names one. Nothing has to cross between parts.
Inputs may be any that keep to these rules, and one draw needn't show every extreme that they name: match is a permutation of the persons; the rows of one trait-file shard (one index of fam) name at most 256 persons of one owner, and exactly 256 of some owner. The tiles of one owner sit at distinct block positions (tile_row_family, tile_cols), and every diagonal block position of the owner is among them. `rel_peer`: among the rows of one device no owner is named more than 64 times.
All inputs are finite; a program needn't handle non-finite values.
Results may differ from a plain program's by a relative error of at most 0.0003.
Values sent between devices are 32-bit elements; how exact they have to be, the bound alone decides.
A program may use at most 64 MiB of HBM per device.

v0:
```python
import jax
import jax.numpy as jnp
from jax import lax
from jax.sharding import PartitionSpec as P

ITERS = 3


PRECISION_HIGH = lax.Precision.HIGHEST


def block_rank(owner, groups):
    marker_flags = (owner[:, None] == jnp.arange(groups, dtype=jnp.int32)[None, :]).astype(
        jnp.int32
    )
    ranks = jnp.cumsum(marker_flags, axis=0) - 1
    return jnp.sum(ranks * marker_flags, axis=1)


def forward_tile_map(solution_values, tiles, trow, tcol, nblocks):
    blocks = solution_values.reshape(nblocks, 64, solution_values.shape[1])
    selected_entries = blocks[tcol]
    operator_products = jnp.einsum(
        "olh,ohj->olj", tiles, selected_entries, precision=PRECISION_HIGH
    )
    marker_flags = (trow[None, :] == jnp.arange(nblocks, dtype=jnp.int32)[:, None]).astype(
        jnp.float32
    )
    return jnp.einsum(
        "fo,ouh->fuh", marker_flags, operator_products, precision=PRECISION_HIGH
    ).reshape(solution_values.shape)


def tile_backward(solution_values, tiles, trow, tcol, nblocks):
    blocks = solution_values.reshape(nblocks, 64, solution_values.shape[1])
    selected_entries = blocks[trow]
    operator_products = jnp.einsum(
        "zxp,zxm->zpm", tiles, selected_entries, precision=PRECISION_HIGH
    )
    marker_flags = (tcol[None, :] == jnp.arange(nblocks, dtype=jnp.int32)[:, None]).astype(
        jnp.float32
    )
    return jnp.einsum(
        "fo,ouh->fuh", marker_flags, operator_products, precision=PRECISION_HIGH
    ).reshape(solution_values.shape)


def total_squares(solution_values):
    return lax.psum(jnp.sum(solution_values * solution_values, axis=0), "fam")


def local(
    pheno,
    match,
    diag_var,
    tiles,
    tile_row_family,
    tile_cols,
    rel_row,
    rel_peer,
    rel_slot,
    rel_weight,
):
    groups = lax.axis_size("fam")
    persons = pheno.shape[0]
    nblocks = persons // 64
    tile_set = tiles.reshape(tiles.shape[0], 64, 64)
    peers = rel_peer[:, 0]
    weights = rel_weight[:, None]
    columns = pheno.shape[1]
    owner = match // persons
    slot = match % persons
    cap = 2 * persons // groups
    dest = owner * cap + block_rank(owner, groups)
    send_vals = jnp.zeros((groups * cap, columns), jnp.float32).at[dest].set(pheno)
    send_slots = jnp.full((groups * cap,), -1.0, jnp.float32).at[dest].set(slot.astype(jnp.float32))
    got_vals, got_slots = (
        lax.all_to_all(send_vals, "fam", split_axis=0, concat_axis=0, tiled=True),
        lax.all_to_all(send_slots, "fam", split_axis=0, concat_axis=0, tiled=True),
    )
    landing = jnp.where(got_slots >= 0, got_slots.astype(jnp.int32), persons)
    target = jnp.zeros((persons, columns), jnp.float32).at[landing].set(got_vals, mode="drop")
    entries = rel_row.shape[0]
    rcap = 2 * entries // groups
    rdest = peers * rcap + block_rank(peers, groups)
    asks = jnp.full((groups * rcap,), -1, jnp.int32).at[rdest].set(rel_slot)
    incoming = lax.all_to_all(asks, "fam", split_axis=0, concat_axis=0, tiled=True)
    valid = incoming >= 0
    picked_slot = jnp.where(valid, incoming, 0)
    arriving = jnp.where(valid, incoming, persons)
    solution_field = jnp.zeros((persons, columns), jnp.float32)
    residual = target
    direction = target
    norm_now = total_squares(residual)
    for step in range(ITERS):
        factor_part = forward_tile_map(direction, tile_set, tile_row_family, tile_cols, nblocks)
        outgoing = jnp.where(valid[:, None], direction[picked_slot], 0.0)
        answers = lax.all_to_all(outgoing, "fam", split_axis=0, concat_axis=0, tiled=True)
        factor_part = factor_part.at[rel_row].add(weights * answers[rdest])
        factor_part = lax.psum(factor_part, "rep")
        part = tile_backward(factor_part, tile_set, tile_row_family, tile_cols, nblocks)
        pushed = (
            jnp.zeros((groups * rcap, columns), jnp.float32)
            .at[rdest]
            .set(weights * factor_part[rel_row])
        )
        landed = lax.all_to_all(pushed, "fam", split_axis=0, concat_axis=0, tiled=True)
        part = part.at[arriving].add(landed, mode="drop")
        part = lax.psum(part, "rep")
        image = diag_var[:, None] * direction + part
        curvature = lax.psum(jnp.sum(direction * image, axis=0), "fam")
        alpha = norm_now / curvature
        solution_field = solution_field + alpha[None, :] * direction
        residual = residual - alpha[None, :] * image
        norm_next = total_squares(residual)
        direction = residual + (norm_next / norm_now)[None, :] * direction
        norm_now = norm_next
    return (solution_field, residual)


def solution(mesh):
    placed = (
        P(("groups", "fam"), "trait"),
        P(("groups", "fam")),
        P(("groups", "fam")),
        P(("groups", "fam", "rep"), None),
        P(("groups", "fam", "rep")),
        P(("groups", "fam", "rep")),
        P(("groups", "fam", "rep")),
        P(("groups", "fam", "rep"), None),
        P(("groups", "fam", "rep")),
        P(("groups", "fam", "rep")),
    )
    return jax.shard_map(
        local,
        mesh=mesh,
        in_specs=placed,
        out_specs=(P(("groups", "fam"), "trait"), P(("groups", "fam"), "trait")),
        check_vma=False,
    )
```

profile of v0, /device:TPU:0, one launch (start us, length us, event | category | flops | bytes accessed | tf_op | source)
XLA Modules:
  0.0 427.9 jit_solution(10934034351632732826)
XLA Ops:
  11.4 6.3 %all-to-all-start.2 = ((s32[4,64,1]{1,2,0:T(1,128)}), s32[4,64,1]{1,2,0:T(1,128)S(1)}, u32[]{:S(2)}, u32[]{:S(2)}) async-start(s32[4,64,1]{1,2,0:T(1,128)} %all_to_all.69), calls=%async_computation.2 | async-start | bytes 4096 | tf_op jit(solution)/shard_map/all_to_all | solution.py:87
  23.1 5.1 %all-to-all-start = ((f32[4,256,1]{1,2,0:T(1,128)}), f32[4,256,1]{1,2,0:T(1,128)S(1)}, u32[]{:S(2)}, u32[]{:S(2)}) async-start(f32[4,256,1]{1,2,0:T(1,128)} %bitcast.2), calls=%async_computation | async-start | bytes 8192 | tf_op jit(solution)/shard_map/all_to_all | solution.py:79
  39.2 45.7 %all-to-all-done.1 = f32[4,256,512]{2,1,0:T(8,128)S(1)} async-done(((f32[4,256,512]{2,1,0:T(8,128)}), f32[4,256,512]{2,1,0:T(8,128)S(1)}, u32[]{:S(2)}, u32[]{:S(2)}) %all-to-all-start.1) | async-done | bytes 2097184 | tf_op jit(solution)/shard_map/all_to_all | solution.py:78
  86.2 5.7 %scatter_custom_fusion.2 = f32[512,512]{1,0:T(8,128)S(1)} fusion(s32[1024]{0:T(1024)S(1)} %bitcast.130, f32[1024,512]{1,0:T(8,128)} %bitcast.115, f32[]{:T(128)} %constant.24.clone.1), kind=kCustom, calls=%fused_computation.63 | custom fusion | bytes 1049088 | tf_op jit(solution)/shard_map/scatter | solution.py:82
  106.4 4.9 %all-to-all-done.3 = f32[4,64,512]{2,1,0:T(8,128)S(1)} async-done(((f32[4,64,512]{2,1,0:T(8,128)}), f32[4,64,512]{2,1,0:T(8,128)S(1)}, u32[]{:S(2)}, u32[]{:S(2)}) %all-to-all-start.3) | async-done | bytes 524320 | tf_op jit(solution)/shard_map/all_to_all | solution.py:98
  114.5 18.8 %all-reduce.8.cloned.1.call-done = f32[512,512]{1,0:T(8,128)} async-done(((f32[512,512]{1,0:T(8,128)}), f32[512,512]{1,0:T(8,128)}) %all-reduce.8.cloned.1.call-update) | async-done | bytes 1048592 | tf_op jit(solution)/shard_map/psum | solution.py:100
  136.5 4.9 %all-to-all-start.4 = ((f32[4,64,512]{2,1,0:T(8,128)}), f32[4,64,512]{2,1,0:T(8,128)S(1)}, u32[]{:S(2)}, u32[]{:S(2)}) async-start(f32[4,64,512]{2,1,0:T(8,128)} %bitcast.119), calls=%async_computation.4 | async-start | bytes 1048576 | tf_op jit(solution)/shard_map/all_to_all | solution.py:107
  149.8 6.6 %all-to-all-done.4 = f32[4,64,512]{2,1,0:T(8,128)S(1)} async-done(((f32[4,64,512]{2,1,0:T(8,128)}), f32[4,64,512]{2,1,0:T(8,128)S(1)}, u32[]{:S(2)}, u32[]{:S(2)}) %all-to-all-start.4) | async-done | bytes 524320 | tf_op jit(solution)/shard_map/all_to_all | solution.py:107
  159.9 18.8 %all-reduce.10.cloned.1.call-done = f32[512,512]{1,0:T(8,128)} async-done(((f32[512,512]{1,0:T(8,128)}), f32[512,512]{1,0:T(8,128)}) %all-reduce.10.cloned.1.call-update) | async-done | bytes 1048592 | tf_op jit(solution)/shard_map/psum | solution.py:109
  180.2 12.0 %all-reduce = (f32[512]{0:T(512)S(1)}, f32[512]{0:T(512)S(1)}) all-reduce(f32[512]{0:T(512)S(1)} %get-tuple-element.3, f32[512]{0:T(512)S(1)} %get-tuple-element.2), channel_id=1, replica_groups=mesh['groups'=2,'fam'=4,'trait'=2,'rep'=2] {'fam'}, use_global_device_ids=true, to_apply=%region_7.8 | all-reduce | flops 1024 | bytes 8192 | tf_op jit(solution)/shard_map/psum | solution.py:49
  192.5 8.4 %psum.88 = f32[512]{0:T(512)S(1)} all-reduce(f32[512]{0:T(512)S(1)} %multiply_reduce_fusion.3), channel_id=1, replica_groups=mesh['groups'=2,'fam'=4,'trait'=2,'rep'=2] {'fam'}, use_global_device_ids=true, to_apply=%region_19.20 | all-reduce | flops 512 | bytes 4096 | tf_op jit(solution)/shard_map/psum | solution.py:49
  223.1 19.0 %all-reduce.12.cloned.1.call-done = f32[512,512]{1,0:T(8,128)} async-done(((f32[512,512]{1,0:T(8,128)}), f32[512,512]{1,0:T(8,128)}) %all-reduce.12.cloned.1.call-update) | async-done | bytes 1048592 | tf_op jit(solution)/shard_map/psum | solution.py:100
  245.4 4.9 %all-to-all-start.6 = ((f32[4,64,512]{2,1,0:T(8,128)}), f32[4,64,512]{2,1,0:T(8,128)}, u32[]{:S(2)}, u32[]{:S(2)}) async-start(f32[4,64,512]{2,1,0:T(8,128)} %bitcast.32), calls=%async_computation.6 | async-start | bytes 1048576 | tf_op jit(solution)/shard_map/all_to_all | solution.py:107
  259.9 5.4 %all-to-all-done.6 = f32[4,64,512]{2,1,0:T(8,128)} async-done(((f32[4,64,512]{2,1,0:T(8,128)}), f32[4,64,512]{2,1,0:T(8,128)}, u32[]{:S(2)}, u32[]{:S(2)}) %all-to-all-start.6) | async-done | bytes 524320 | tf_op jit(solution)/shard_map/all_to_all | solution.py:107
  269.3 18.8 %all-reduce.14.cloned.1.call-done = f32[512,512]{1,0:T(8,128)} async-done(((f32[512,512]{1,0:T(8,128)}), f32[512,512]{1,0:T(8,128)}) %all-reduce.14.cloned.1.call-update) | async-done | bytes 1048592 | tf_op jit(solution)/shard_map/psum | solution.py:109
  289.5 12.0 %psum.91 = f32[512]{0:T(512)S(1)} all-reduce(f32[512]{0:T(512)S(1)} %multiply_reduce_fusion.2), channel_id=1, replica_groups=mesh['groups'=2,'fam'=4,'trait'=2,'rep'=2] {'fam'}, use_global_device_ids=true, to_apply=%region_26.27 | all-reduce | flops 512 | bytes 4096 | tf_op jit(solution)/shard_map/psum | solution.py:111
  304.1 8.3 %psum.92 = f32[512]{0:T(512)S(1)} all-reduce(f32[512]{0:T(512)S(1)} %get-tuple-element.6), channel_id=1, replica_groups=mesh['groups'=2,'fam'=4,'trait'=2,'rep'=2] {'fam'}, use_global_device_ids=true, to_apply=%region_28.29 | all-reduce | flops 512 | bytes 4096 | tf_op jit(solution)/shard_map/psum | solution.py:49
  333.3 4.9 %scatter_custom_fusion.10 = f32[512,512]{1,0:T(8,128)} fusion(f32[512,512]{1,0:T(8,128)} %bitcast.108, s32[128]{0:T(128)S(1)} %compare_select_fusion.9, f32[128]{0:T(128)S(1)} %copy-done.10, f32[256,512]{1,0:T(8,128)} %bitcast.38, s32[1024]{0:T(1024)S(1)} %pad_clamp_fusion.2), kind=kCustom, calls=%fused_computation.67 | custom fusion | flops 131072 | bytes 1577472 | tf_op jit(solution)/shard_map/scatter-add | solution.py:99
  338.3 19.3 %all-reduce.16.cloned.1.call-done = f32[512,512]{1,0:T(8,128)} async-done(((f32[512,512]{1,0:T(8,128)}), f32[512,512]{1,0:T(8,128)}) %all-reduce.16.cloned.1.call-update) | async-done | bytes 1048592 | tf_op jit(solution)/shard_map/psum | solution.py:100
  360.8 4.9 %all-to-all-start.8 = ((f32[4,64,512]{2,1,0:T(8,128)}), f32[4,64,512]{2,1,0:T(8,128)}, u32[]{:S(2)}, u32[]{:S(2)}) async-start(f32[4,64,512]{2,1,0:T(8,128)} %bitcast.118), calls=%async_computation.8 | async-start | bytes 1048576 | tf_op jit(solution)/shard_map/all_to_all | solution.py:107
  376.3 4.4 %all-to-all-done.8 = f32[4,64,512]{2,1,0:T(8,128)} async-done(((f32[4,64,512]{2,1,0:T(8,128)}), f32[4,64,512]{2,1,0:T(8,128)}, u32[]{:S(2)}, u32[]{:S(2)}) %all-to-all-start.8) | async-done | bytes 524320 | tf_op jit(solution)/shard_map/all_to_all | solution.py:107
  380.7 4.7 %scatter_fusion.2 = f32[512,512]{1,0:T(8,128)} fusion(f32[512,512]{1,0:T(8,128)} %bitcast.103, s32[256]{0:T(256)S(1)} %bitcast.123, f32[256,512]{1,0:T(8,128)} %bitcast.43), kind=kCustom, calls=%fused_computation.27 | custom fusion | flops 131072 | bytes 1573888 | tf_op jit(solution)/shard_map/scatter-add | solution.py:108
  385.5 18.8 %all-reduce.18.cloned.1.call-done = f32[512,512]{1,0:T(8,128)} async-done(((f32[512,512]{1,0:T(8,128)}), f32[512,512]{1,0:T(8,128)}) %all-reduce.18.cloned.1.call-update) | async-done | bytes 1048592 | tf_op jit(solution)/shard_map/psum | solution.py:109
  405.7 12.0 %psum.95 = f32[512]{0:T(512)S(1)} all-reduce(f32[512]{0:T(512)S(1)} %multiply_reduce_fusion), channel_id=1, replica_groups=mesh['groups'=2,'fam'=4,'trait'=2,'rep'=2] {'fam'}, use_global_device_ids=true, to_apply=%region_35.36 | all-reduce | flops 512 | bytes 4096 | tf_op jit(solution)/shard_map/psum | solution.py:111
  (131 shorter events, 138.7 us)
Async XLA Ops:
  11.4 11.8 %all-to-all-start.2 = ((s32[4,64,1]{1,2,0:T(1,128)}), s32[4,64,1]{1,2,0:T(1,128)S(1)}, u32[]{:S(2)}, u32[]{:S(2)}) async-start(s32[4,64,1]{1,2,0:T(1,128)} %all_to_all.69), calls=%async_computation.2 | async-start | bytes 4096 | tf_op jit(solution)/shard_map/all_to_all | solution.py:87
  23.1 10.6 %all-to-all-start = ((f32[4,256,1]{1,2,0:T(1,128)}), f32[4,256,1]{1,2,0:T(1,128)S(1)}, u32[]{:S(2)}, u32[]{:S(2)}) async-start(f32[4,256,1]{1,2,0:T(1,128)} %bitcast.2), calls=%async_computation | async-start | bytes 8192 | tf_op jit(solution)/shard_map/all_to_all | solution.py:79
  33.8 4.0 copy-start.13
  33.8 4.0 copy-start.12
  33.8 51.1 %all-to-all-start.1 = ((f32[4,256,512]{2,1,0:T(8,128)}), f32[4,256,512]{2,1,0:T(8,128)S(1)}, u32[]{:S(2)}, u32[]{:S(2)}) async-start(f32[4,256,512]{2,1,0:T(8,128)} %bitcast.5), calls=%async_computation.1 | async-start | bytes 4194304 | tf_op jit(solution)/shard_map/all_to_all | solution.py:78
  92.9 5.0 %copy-start.8 = (f32[16,4096]{1,0:T(8,128)S(1)}, f32[16,4096]{1,0:T(8,128)}, u32[]{:S(2)}) copy-start(f32[16,4096]{1,0:T(8,128)} %param.13) | copy-start | bytes 786436
  93.8 17.4 %all-to-all-start.3 = ((f32[4,64,512]{2,1,0:T(8,128)}), f32[4,64,512]{2,1,0:T(8,128)S(1)}, u32[]{:S(2)}, u32[]{:S(2)}) async-start(f32[4,64,512]{2,1,0:T(8,128)} %broadcast_select_fusion.2), calls=%async_computation.3 | async-start | bytes 1048576 | tf_op jit(solution)/shard_map/all_to_all | solution.py:98
  97.3 36.0 %all-reduce.8.cloned.1.call-start = ((), (), s32[]{:S(2)}) async-start(), calls=%async_computation.9 | async-start | bytes 2097152 | tf_op jit(solution)/shard_map/psum | solution.py:100
  98.1 155.6 %copy-start.2 = (f32[16,64,64]{2,1,0:T(8,128)}, f32[16,64,64]{2,1,0:T(8,128)S(1)}, u32[]{:S(2)}) copy-start(f32[16,64,64]{2,1,0:T(8,128)S(1)} %reshape.200) | copy-start | bytes 786436
  103.8 7.5 %copy-start.10 = (f32[128]{0:T(128)S(1)}, f32[128]{0:T(128)}, u32[]{:S(2)}) copy-start(f32[128]{0:T(128)} %param.19) | copy-start | bytes 1540
  133.3 8.3 %copy-start.5 = (f32[512,512]{1,0:T(8,128)S(1)}, f32[512,512]{1,0:T(8,128)}, u32[]{:S(2)}) copy-start(f32[512,512]{1,0:T(8,128)} %all-reduce.8.cloned.1.call-done) | copy-start | bytes 3145732
  136.5 19.8 %all-to-all-start.4 = ((f32[4,64,512]{2,1,0:T(8,128)}), f32[4,64,512]{2,1,0:T(8,128)S(1)}, u32[]{:S(2)}, u32[]{:S(2)}) async-start(f32[4,64,512]{2,1,0:T(8,128)} %bitcast.119), calls=%async_computation.4 | async-start | bytes 1048576 | tf_op jit(solution)/shard_map/all_to_all | solution.py:107
  141.4 37.2 %all-reduce.10.cloned.1.call-start = ((), (), s32[]{:S(2)}) async-start(), calls=%async_computation.10 | async-start | bytes 2097152 | tf_op jit(solution)/shard_map/psum | solution.py:109
  156.4 22.3 %copy-start.9 = (f32[512]{0:T(512)S(1)}, f32[512]{0:T(512)}, u32[]{:S(2)}) copy-start(f32[512]{0:T(512)} %param.12) | copy-start | bytes 6148
  178.7 13.5 %copy-start.3 = (f32[512,512]{1,0:T(8,128)S(1)}, f32[512,512]{1,0:T(8,128)}, u32[]{:S(2)}) copy-start(f32[512,512]{1,0:T(8,128)} %all-reduce.10.cloned.1.call-done) | copy-start | bytes 3145732
  204.3 14.9 %all-to-all-start.5 = ((f32[4,64,512]{2,1,0:T(8,128)}), f32[4,64,512]{2,1,0:T(8,128)S(1)}, u32[]{:S(2)}, u32[]{:S(2)}) async-start(f32[4,64,512]{2,1,0:T(8,128)} %broadcast_select_fusion.1), calls=%async_computation.5 | async-start | bytes 1048576 | tf_op jit(solution)/shard_map/all_to_all | solution.py:98
  207.7 34.4 %all-reduce.12.cloned.1.call-start = ((), (), s32[]{:S(2)}) async-start(), calls=%async_computation.11 | async-start | bytes 2097152 | tf_op jit(solution)/shard_map/psum | solution.py:100
  245.4 19.9 %all-to-all-start.6 = ((f32[4,64,512]{2,1,0:T(8,128)}), f32[4,64,512]{2,1,0:T(8,128)}, u32[]{:S(2)}, u32[]{:S(2)}) async-start(f32[4,64,512]{2,1,0:T(8,128)} %bitcast.32), calls=%async_computation.6 | async-start | bytes 1048576 | tf_op jit(solution)/shard_map/all_to_all | solution.py:107
  250.3 37.8 %all-reduce.14.cloned.1.call-start = ((), (), s32[]{:S(2)}) async-start(), calls=%async_computation.12 | async-start | bytes 2097152 | tf_op jit(solution)/shard_map/psum | solution.py:109
  269.3 32.2 %copy-start.4 = (f32[512,512]{1,0:T(8,128)S(1)}, f32[512,512]{1,0:T(8,128)}, u32[]{:S(2)}) copy-start(f32[512,512]{1,0:T(8,128)} %all-reduce.10.cloned.1.call-done) | copy-start | bytes 3145732
  317.6 15.7 %all-to-all-start.7 = ((f32[4,64,512]{2,1,0:T(8,128)}), f32[4,64,512]{2,1,0:T(8,128)}, u32[]{:S(2)}, u32[]{:S(2)}) async-start(f32[4,64,512]{2,1,0:T(8,128)} %broadcast_select_fusion), calls=%async_computation.7 | async-start | bytes 1048576 | tf_op jit(solution)/shard_map/all_to_all | solution.py:98
  321.8 35.7 %all-reduce.16.cloned.1.call-start = ((), (), s32[]{:S(2)}) async-start(), calls=%async_computation.13 | async-start | bytes 2097152 | tf_op jit(solution)/shard_map/psum | solution.py:100
  360.8 19.9 %all-to-all-start.8 = ((f32[4,64,512]{2,1,0:T(8,128)}), f32[4,64,512]{2,1,0:T(8,128)}, u32[]{:S(2)}, u32[]{:S(2)}) async-start(f32[4,64,512]{2,1,0:T(8,128)} %bitcast.118), calls=%async_computation.8 | async-start | bytes 1048576 | tf_op jit(solution)/shard_map/all_to_all | solution.py:107
  365.7 38.6 %all-reduce.18.cloned.1.call-start = ((), (), s32[]{:S(2)}) async-start(), calls=%async_computation.14 | async-start | bytes 2097152 | tf_op jit(solution)/shard_map/psum | solution.py:109
  (5 other events, 7.8 us)
Sparse Core Ops, SparseCore 0:
  114.6 18.6 all-reduce.7
  160.0 18.6 all-reduce.9
  223.2 18.8 all-reduce.11
  269.4 18.6 all-reduce.13
  338.4 19.0 all-reduce.15
  385.6 18.6 all-reduce.17
where the time goes:
time: 435 us; the launch traced here: 428 us
  waiting for transfers between devices  186 us (43%)
  other arithmetic  53.6 us (12%)
  blocking collectives  52.6 us (12%)
  local copies, waits for them, and re-layouts  45.1 us (10%)
  starting transfers between devices  43 us (10%)
  matrix products  33.2 us (8%)
  between operations  14.7 us (3%)
    psum x3, waiting for transfers between devices, local(): factor_part = lax.psum(factor_part, 'rep')  57.1 us
    psum x3, waiting for transfers between devices, local(): part = lax.psum(part, 'rep')  56.4 us
    all_to_all x1, waiting for transfers between devices, local(): lax.all_to_all(send_vals, 'fam', split_axis=0, concat_axis=0, tiled=True)  45.7 us
    psum x3, blocking collectives, total_squares(): return lax.psum(jnp.sum(solution_values * solution_values, axis=0), 'fam')  28.7 us
    psum x2, blocking collectives, local(): curvature = lax.psum(jnp.sum(direction * image, axis=0), 'fam')  23.9 us
    all_to_all x3, waiting for transfers between devices, local(): lax.all_to_all(pushed, 'fam', split_axis=0, concat_axis=0, tiled=True)  16.4 us
    all_to_all x3, starting transfers between devices, local(): lax.all_to_all(pushed, 'fam', split_axis=0, concat_axis=0, tiled=True)  14.6 us
    all_to_all x3, starting transfers between devices, local(): lax.all_to_all(outgoing, 'fam', split_axis=0, concat_axis=0, tiled=True)  11.1 us
  transfers between devices with their start and end apart: 15, of which 14 were waited for; matrix products, arithmetic and copies ran while one was open for 15% of the time, Pallas kernels for 0%

commit v1 on v0

--- a/solution.py
+++ b/solution.py
@@ -1,6 +1,10 @@
+import functools
+
 import jax
 import jax.numpy as jnp
 from jax import lax
+from jax.experimental import pallas as pl
+from jax.experimental.pallas import tpu as pltpu
 from jax.sharding import PartitionSpec as P
 
 ITERS = 3
@@ -118,6 +122,293 @@
     return (solution_field, residual)
 
 
+def split_terms(values):
+    high = values.astype(jnp.bfloat16)
+    low = (values - high.astype(jnp.float32)).astype(jnp.bfloat16)
+    return jnp.concatenate([high, low], axis=1)
+
+
+def fold(values):
+    half = values.shape[1] // 2
+    return values[:, :half] + values[:, half:]
+
+
+def mm(left, right):
+    return jnp.dot(left, right, preferred_element_type=jnp.float32)
+
+
+def one_hot_rows(ref, index_col, rows, strip):
+    width = ref.shape[1]
+
+    def body(i, _):
+        at = pl.ds(pl.multiple_of(i * strip, strip), strip)
+        lane = lax.broadcasted_iota(jnp.int32, (strip, width), 1)
+        ref[at, :] = jnp.where(index_col[at, :] == lane, 1.0, 0.0).astype(jnp.bfloat16)
+        return 0
+
+    lax.fori_loop(0, rows // strip, body, 0)
+
+
+def one_hot_cols(ref, index_row, rows, strip):
+    width = ref.shape[1]
+
+    def body(i, _):
+        at = pl.ds(pl.multiple_of(i * strip, strip), strip)
+        sub = lax.broadcasted_iota(jnp.int32, (strip, width), 0) + i * strip
+        ref[at, :] = jnp.where(index_row[...] == sub, 1.0, 0.0).astype(jnp.bfloat16)
+        return 0
+
+    lax.fori_loop(0, rows // strip, body, 0)
+
+
+def build_factor(owners, per_owner, nblk, trow, tcol, tiles, kb, ktb, khi, klo, kthi, ktlo):
+    def owner(o, _):
+        kb[...] = jnp.zeros_like(kb)
+        ktb[...] = jnp.zeros_like(ktb)
+
+        def place(t, _):
+            e = o * per_owner + t
+            pair = tiles[e]
+            tile = jnp.concatenate([pair[:, :64], pair[:, 64:]], axis=0)
+            a, b = trow[e], tcol[e]
+            kb[b, pl.ds(pl.multiple_of(a * 64, 64), 64), :] = tile
+            ktb[a, pl.ds(pl.multiple_of(b * 64, 64), 64), :] = tile.T
+            return 0
+
+        lax.fori_loop(0, per_owner, place, 0)
+        for src, hi, lo in ((kb, khi, klo), (ktb, kthi, ktlo)):
+            full = jnp.concatenate([src[j] for j in range(nblk)], axis=1)
+            high = full.astype(jnp.bfloat16)
+            hi[o] = high
+            lo[o] = (full - high.astype(jnp.float32)).astype(jnp.bfloat16)
+        return 0
+
+    lax.fori_loop(0, owners, owner, 0)
+
+
+def group_kernel(
+    owners,
+    persons,
+    per_owner,
+    trow,
+    tcol,
+    me_ref,
+    tiles,
+    match_row,
+    diag,
+    col_row,
+    col_col,
+    row_row,
+    row_col,
+    weight,
+    pheno,
+    x_out,
+    r_out,
+    kb,
+    ktb,
+    khi,
+    klo,
+    kthi,
+    ktlo,
+    pm,
+    c,
+    ct,
+    rsel,
+    rselt,
+    d,
+    r,
+    dcat,
+    ycat,
+    hcat,
+):
+    every = owners * persons
+    entries = c.shape[0]
+    eown = entries // owners
+    n = pheno.shape[1]
+    nblk = persons // 64
+    me = me_ref[0]
+
+    @pl.when(pl.program_id(0) == 0)
+    def _():
+        build_factor(
+            owners, per_owner, nblk, trow, tcol, tiles, kb, ktb, khi, klo, kthi, ktlo
+        )
+        one_hot_cols(pm, match_row, every, 64)
+        one_hot_rows(c, col_col, entries, 64)
+        one_hot_cols(ct, col_row, every, 64)
+        one_hot_rows(rsel, row_col, entries, 64)
+        for o in range(owners):
+            lane = row_row[:, o * eown : (o + 1) * eown]
+            sub = lax.broadcasted_iota(jnp.int32, (persons, eown), 0)
+            rselt[o] = jnp.where(lane == sub, 1.0, 0.0).astype(jnp.bfloat16)
+
+    def person(o):
+        return pl.ds(pl.multiple_of(o * persons, persons), persons)
+
+    def entry(o):
+        return pl.ds(pl.multiple_of(o * eown, eown), eown)
+
+    zero = jnp.zeros((1, n), jnp.float32)
+
+    def colsum(v):
+        return jnp.sum(v, axis=0, keepdims=True)
+
+    ycat[...] = split_terms(pheno[...])
+
+    def begin(o, carry):
+        rr, dd = carry
+        t = fold(mm(pm[person(o), :], ycat[...]))
+        r[person(o), :] = t
+        d[person(o), :] = t
+        dcat[person(o), :] = split_terms(t)
+        square = t * t
+        return rr + colsum(square), dd + colsum(square * diag[person(o), :])
+
+    rr, dd = lax.fori_loop(0, owners, begin, (zero, zero))
+
+    def forward(o, yy):
+        g = fold(mm(c[entry(o), :], dcat[...])) * weight[entry(o), :]
+        near = dcat[person(o), :]
+        y = fold(mm(khi[o], near) + mm(rselt[o], split_terms(g)))
+        y = y + mm(klo[o], near[:, :n])
+        ys = split_terms(y)
+        ycat[person(o), :] = ys
+        h = fold(mm(rsel[entry(o), :], ys)) * weight[entry(o), :]
+        hcat[entry(o), :] = split_terms(h)
+        return yy + colsum(y * y)
+
+    def image(o):
+        ys = ycat[person(o), :]
+        back = fold(mm(kthi[o], ys) + mm(ct[person(o), :], hcat[...]))
+        back = back + mm(ktlo[o], ys[:, :n])
+        return diag[person(o), :] * d[person(o), :] + back
+
+    for step in range(ITERS):
+        yy = lax.fori_loop(0, owners, forward, zero)
+        alpha = rr / (yy + dd)
+        move = alpha * d[person(me), :]
+        if step == 0:
+            x_out[...] = move
+        else:
+            x_out[...] = x_out[...] + move
+        if step == ITERS - 1:
+            r_out[...] = r[person(me), :] - alpha * image(me)
+            break
+
+        def descend(o, acc):
+            left = r[person(o), :] - alpha * image(o)
+            r[person(o), :] = left
+            return acc + colsum(left * left)
+
+        nxt = lax.fori_loop(0, owners, descend, zero)
+        beta = nxt / rr
+        rr = nxt
+
+        def turn(o, acc):
+            v = r[person(o), :] + beta * d[person(o), :]
+            d[person(o), :] = v
+            dcat[person(o), :] = split_terms(v)
+            return acc + colsum(v * v * diag[person(o), :])
+
+        dd = lax.fori_loop(0, owners, turn, zero)
+
+
+def local_group(
+    pheno,
+    match,
+    diag_var,
+    tiles,
+    tile_row_family,
+    tile_cols,
+    rel_row,
+    rel_peer,
+    rel_slot,
+    rel_weight,
+):
+    owners = lax.axis_size("fam")
+    reps = lax.axis_size("rep")
+    traits = lax.axis_size("trait")
+    persons, columns = pheno.shape
+    mine = columns // reps
+    n = 128
+    me = lax.axis_index("fam")
+    rep = lax.axis_index("rep")
+    held = tiles.shape[0]
+    share = held // traits
+    pairs = tiles.reshape(held, 32, 128)
+    pairs = lax.dynamic_slice_in_dim(pairs, lax.axis_index("trait") * share, share, 0)
+    pairs = lax.all_gather(pairs, ("fam", "rep", "trait"), tiled=True)
+    col = rel_peer[:, 0] * persons + rel_slot
+    inner = rel_row % 64
+    row = rel_row - inner + (inner % 2) * 32 + inner // 2
+    ints = (match, tile_row_family, tile_cols, col, row)
+    packed = jnp.concatenate([v.astype(jnp.float32) for v in ints] + [diag_var, rel_weight])
+    everyone = lax.all_gather(packed, ("fam", "rep")).reshape(owners, reps, -1)
+    sizes = [v.shape[0] for v in ints] + [persons, rel_row.shape[0]]
+    parts, at = [], 0
+    for size in sizes:
+        parts.append(everyone[:, :, at : at + size])
+        at += size
+    match_all = parts[0][:, 0].reshape(1, -1).astype(jnp.int32)
+    trow = parts[1].reshape(-1).astype(jnp.int32)
+    tcol = parts[2].reshape(-1).astype(jnp.int32)
+    col_all = parts[3].reshape(-1).astype(jnp.int32)
+    row_all = parts[4].reshape(-1).astype(jnp.int32)
+    diag_all = parts[5][:, 0].reshape(-1, 1)
+    weight_all = parts[6].reshape(-1, 1)
+    part = lax.dynamic_slice_in_dim(pheno, rep * mine, mine, 1)
+    gathered = lax.all_gather(part, "fam", tiled=True)
+    every = owners * persons
+    entries = col_all.shape[0]
+    eown = entries // owners
+    nblk = persons // 64
+    smem = pl.BlockSpec(memory_space=pltpu.SMEM)
+    vmem = pl.BlockSpec(memory_space=pltpu.VMEM)
+    bf = jnp.bfloat16
+    x, r = pl.pallas_call(
+        functools.partial(group_kernel, owners, persons, held * reps),
+        grid=(mine // n,),
+        out_shape=[jax.ShapeDtypeStruct((persons, mine), jnp.float32)] * 2,
+        in_specs=[smem] * 3 + [vmem] * 8 + [pl.BlockSpec((every, n), lambda i: (0, i))],
+        out_specs=[pl.BlockSpec((persons, n), lambda i: (0, i))] * 2,
+        scratch_shapes=[
+            pltpu.VMEM((nblk, persons, 64), jnp.float32),
+            pltpu.VMEM((nblk, persons, 64), jnp.float32),
+            pltpu.VMEM((owners, persons, persons), bf),
+            pltpu.VMEM((owners, persons, persons), bf),
+            pltpu.VMEM((owners, persons, persons), bf),
+            pltpu.VMEM((owners, persons, persons), bf),
+            pltpu.VMEM((every, every), bf),
+            pltpu.VMEM((entries, every), bf),
+            pltpu.VMEM((every, entries), bf),
+            pltpu.VMEM((entries, persons), bf),
+            pltpu.VMEM((owners, persons, eown), bf),
+            pltpu.VMEM((every, n), jnp.float32),
+            pltpu.VMEM((every, n), jnp.float32),
+            pltpu.VMEM((every, 2 * n), bf),
+            pltpu.VMEM((every, 2 * n), bf),
+            pltpu.VMEM((entries, 2 * n), bf),
+        ],
+        compiler_params=pltpu.CompilerParams(vmem_limit_bytes=60 * 2**20),
+    )(
+        trow,
+        tcol,
+        me.reshape(1),
+        pairs,
+        match_all,
+        diag_all,
+        col_all.reshape(1, -1),
+        col_all.reshape(-1, 1),
+        row_all.reshape(1, -1),
+        row_all.reshape(-1, 1),
+        weight_all,
+        gathered,
+    )
+    x = lax.all_gather(x, "rep", axis=1, tiled=True)
+    r = lax.all_gather(r, "rep", axis=1, tiled=True)
+    return x, r
+
+
 def solution(mesh):
     placed = (
         P(("groups", "fam"), "trait"),
@@ -131,8 +422,9 @@
         P(("groups", "fam", "rep")),
         P(("groups", "fam", "rep")),
     )
+    whole = mesh.shape["fam"] <= 4
     return jax.shard_map(
-        local,
+        local_group if whole else local,
         mesh=mesh,
         in_specs=placed,
         out_specs=(P(("groups", "fam"), "trait"), P(("groups", "fam"), "trait")),

time: 435 us -> 221 us (0.51)
  the two profiles are of different devices: /device:TPU:0 before, /device:TPU:25 now
where the time goes in v1:
time: 221 us; the launch traced here: 220 us
  Pallas kernels  89.6 us (41%)
  waiting for transfers between devices  73.5 us (33%)
  blocking collectives  27.3 us (12%)
  between operations  14.6 us (7%)
  local copies, waits for them, and re-layouts  13.8 us (6%)
    pallas_call x1, Pallas kernels, local_group(): pl.pallas_call(functools.partial(group_kernel, owners, persons, held * re...  89.6 us
    all_gather x1, waiting for transfers between devices, local_group(): pairs = lax.all_gather(pairs, ('fam', 'rep', 'trait'), tiled=True)  43.8 us
    unnamed x1, blocking collectives  27.3 us
    all_gather x1, waiting for transfers between devices, local_group(): r = lax.all_gather(r, 'rep', axis=1, tiled=True)  11.6 us
    all_gather x1, waiting for transfers between devices, local_group(): x = lax.all_gather(x, 'rep', axis=1, tiled=True)  8.92 us
    all_gather x1, waiting for transfers between devices, local_group(): gathered = lax.all_gather(part, 'fam', tiled=True)  8.57 us
    unnamed x32, local copies, waits for them, and re-layouts  6.42 us
  transfers between devices with their start and end apart: 4, of which 4 were waited for; matrix products, arithmetic and copies ran while one was open for 4% of the time, Pallas kernels for 0%

profile of v1, /device:TPU:25, one launch (start us, length us, event | category | flops | bytes accessed | tf_op | source)
XLA Modules:
  0.0 219.8 jit_solution(7536708541462422749)
XLA Ops:
  7.3 1.1 copy-done
  8.4 0.8 constant_dynamic-slice_fusion
  9.4 1.0 copy.20
  10.4 0.7 constant_dynamic-slice_fusion.1
  11.2 0.6 dynamic-slice
  12.5 0.1 concatenate.3
  12.6 0.3 dynamic-update-slice
  12.9 27.3 %all-reduce = f32[11520]{0:T(1024)S(1)} all-reduce(f32[11520]{0:T(1024)S(1)} %dynamic-update-slice), channel_id=2, replica_groups=mesh['groups'=2,'fam'=4,'trait'=2,'rep'=2] {'fam','rep'}, use_global_device_ids=true, to_apply=%add | all-reduce | flops 11520 | bytes 92160
  40.2 0.1 reshape.85
  40.4 0.7 convert_element_type.84.tcol
  41.1 0.6 convert_element_type.82.trow
  41.8 1.0 copy.19.weight
  42.8 1.0 copy.17.col_col
  43.9 1.0 copy.18.row_col
  44.9 0.6 fusion.7
  45.5 1.3 copy.16.diag
  46.8 8.6 %all-gather.8.cloned.1.call-done.pheno = f32[2048,256]{1,0:T(8,128)} async-done(((f32[512,256]{1,0:T(8,128)}), f32[2048,256]{1,0:T(8,128)}) %all-gather.8.cloned.1.call-update) | async-done | bytes 2097168 | tf_op jit(solution)/shard_map/all_gather | solution.py:360
  55.4 43.8 %all-gather.6.cloned.1.call-done.tiles = f32[128,32,128]{2,1,0:T(8,128)} async-done(((f32[8,32,128]{2,1,0:T(8,128)}), f32[128,32,128]{2,1,0:T(8,128)}) %all-gather.6.cloned.1.call-update) | async-done | bytes 2097168 | tf_op jit(solution)/shard_map/all_gather | solution.py:340
  99.2 89.6 %shard_map.113 = (f32[512,256]{1,0:T(8,128)}, f32[512,256]{1,0:T(8,128)}) custom-call(s32[128]{0:T(128)} %convert_element_type.82.trow, s32[128]{0:T(128)} %convert_element_type.84.tcol, s32[1]{0:T(128)} %bitcast.2.me_ref, f32[128,32,128]{2,1,0:T(8,128)} %all-gather.6.cloned.1.call-done.tiles, s32[1,2048]{1,0:T(1,128)} %bitcast.21, f32[2048,1]{1,0:T(8,128)} %copy.16.diag, ...), custom_call_target="tpu_custom_call" | custom-call | tf_op jit(solution)/shard_map/pallas_call | solution.py:368
  188.9 0.5 all-gather.12.cloned.1.call-update
  189.4 8.9 %all-gather.10.cloned.1.call-done = f32[512,512]{1,0:T(8,128)} async-done(((f32[512,256]{1,0:T(8,128)}), f32[512,512]{1,0:T(8,128)}) %all-gather.10.cloned.1.call-update) | async-done | bytes 1048592 | tf_op jit(solution)/shard_map/all_gather | solution.py:407
  198.3 11.6 %all-gather.12.cloned.1.call-done = f32[512,512]{1,0:T(8,128)} async-done(((f32[512,256]{1,0:T(8,128)}), f32[512,512]{1,0:T(8,128)}) %all-gather.12.cloned.1.call-update) | async-done | bytes 1048592 | tf_op jit(solution)/shard_map/all_gather | solution.py:408
  210.0 2.4 %copy.24 = f32[512,512]{1,0:T(8,128)} copy(f32[512,512]{1,0:T(8,128)} %all-gather.10.cloned.1.call-done) | data formatting | bytes 2097152
  212.3 1.0 copy.25
  (39 shorter events, 0.5 us)
Async XLA Ops:
  7.2 1.3 copy-start
  7.2 4.0 %copy-start.12 = (u32[32]{0:T(128)S(1)}, u32[32]{0:T(128)}, u32[]{:S(2)}) copy-start(u32[32]{0:T(128)} %constant.62) | copy-start | bytes 388
  7.2 3.9 %copy-start.10 = (s32[16]{0:T(128)S(1)}, s32[16]{0:T(128)}, u32[]{:S(2)}) copy-start(s32[16]{0:T(128)} %param.14) | copy-start | bytes 196
  7.2 3.9 %copy-start.11 = (s32[16]{0:T(128)S(1)}, s32[16]{0:T(128)}, u32[]{:S(2)}) copy-start(s32[16]{0:T(128)} %param.15) | copy-start | bytes 196
  7.2 3.9 %copy-start.4 = (s32[512]{0:T(512)S(1)}, s32[512]{0:T(512)}, u32[]{:S(2)}) copy-start(s32[512]{0:T(512)} %param.11) | copy-start | bytes 6148
  7.2 5.2 %copy-start.6 = (s32[128]{0:T(128)S(1)}, s32[128]{0:T(128)}, u32[]{:S(2)}) copy-start(s32[128]{0:T(128)} %param.18) | copy-start | bytes 1540
  7.2 5.2 %copy-start.7 = (s32[128,1]{0,1:T(1,128)S(1)}, s32[128,1]{0,1:T(1,128)}, u32[]{:S(2)}) copy-start(s32[128,1]{0,1:T(1,128)} %param.17) | copy-start | bytes 1540
  7.2 5.2 %copy-start.8 = (s32[128]{0:T(128)S(1)}, s32[128]{0:T(128)}, u32[]{:S(2)}) copy-start(s32[128]{0:T(128)} %param.16) | copy-start | bytes 1540
  7.3 5.2 %copy-start.9 = (f32[128]{0:T(128)S(1)}, f32[128]{0:T(128)}, u32[]{:S(2)}) copy-start(f32[128]{0:T(128)} %param.19) | copy-start | bytes 1540
  7.3 5.2 %copy-start.5 = (f32[512]{0:T(512)S(1)}, f32[512]{0:T(512)}, u32[]{:S(2)}) copy-start(f32[512]{0:T(512)} %param.12) | copy-start | bytes 6148
  7.3 48.1 %all-gather.8.cloned.1.call-start = ((), (), s32[]{:S(2)}) async-start(), calls=%async_computation.1 | async-start | bytes 2621440 | tf_op jit(solution)/shard_map/all_gather | solution.py:360
  9.3 89.9 %all-gather.6.cloned.1.call-start = ((), (), s32[]{:S(2)}) async-start(), calls=%async_computation | async-start | bytes 2228224 | tf_op jit(solution)/shard_map/all_gather | solution.py:340
  11.1 187.3 %all-gather.10.cloned.1.call-start = ((), (), s32[]{:S(2)}) async-start(), calls=%async_computation.2 | async-start | bytes 1572864 | tf_op jit(solution)/shard_map/all_gather | solution.py:407
  41.8 57.5 %copy-start.2 = (s32[4,2,128]{2,1,0:T(2,128)}, s32[4,2,128]{2,1,0:T(2,128)S(1)}, u32[]{:S(2)}) copy-start(s32[4,2,128]{2,1,0:T(2,128)S(1)} %get-tuple-element.7) | copy-start | bytes 12292
  41.8 57.4 %copy-start.3 = (s32[4,2,128]{2,1,0:T(2,128)}, s32[4,2,128]{2,1,0:T(2,128)S(1)}, u32[]{:S(2)}) copy-start(s32[4,2,128]{2,1,0:T(2,128)S(1)} %get-tuple-element.8) | copy-start | bytes 12292
  188.8 21.1 %all-gather.12.cloned.1.call-start = ((), (), s32[]{:S(2)}) async-start(), calls=%async_computation.3 | async-start | bytes 1572864 | tf_op jit(solution)/shard_map/all_gather | solution.py:408
  210.0 2.4 %copy-start.1 = (f32[512,512]{1,0:T(8,128)S(1)}, f32[512,512]{1,0:T(8,128)}, u32[]{:S(2)}) copy-start(f32[512,512]{1,0:T(8,128)} %all-gather.12.cloned.1.call-done) | copy-start | bytes 3145732
Sparse Core Ops, SparseCore 0:
  9.7 45.6 all-gather.7
  57.6 41.5 all-gather.5
  188.9 9.3 all-gather.9
  199.7 10.1 all-gather.11

commit v2 on v1

--- a/solution.py
+++ b/solution.py
@@ -161,51 +161,39 @@
     lax.fori_loop(0, rows // strip, body, 0)
 
 
-def build_factor(owners, per_owner, nblk, trow, tcol, tiles, kb, ktb, khi, klo, kthi, ktlo):
-    def owner(o, _):
-        kb[...] = jnp.zeros_like(kb)
-        ktb[...] = jnp.zeros_like(ktb)
-
-        def place(t, _):
-            e = o * per_owner + t
-            pair = tiles[e]
-            tile = jnp.concatenate([pair[:, :64], pair[:, 64:]], axis=0)
-            a, b = trow[e], tcol[e]
-            kb[b, pl.ds(pl.multiple_of(a * 64, 64), 64), :] = tile
-            ktb[a, pl.ds(pl.multiple_of(b * 64, 64), 64), :] = tile.T
-            return 0
-
-        lax.fori_loop(0, per_owner, place, 0)
-        for src, hi, lo in ((kb, khi, klo), (ktb, kthi, ktlo)):
-            full = jnp.concatenate([src[j] for j in range(nblk)], axis=1)
-            high = full.astype(jnp.bfloat16)
-            hi[o] = high
-            lo[o] = (full - high.astype(jnp.float32)).astype(jnp.bfloat16)
-        return 0
-
-    lax.fori_loop(0, owners, owner, 0)
+def copy_to(src, dst, sems, at, **where):
+    send, recv = sems
+    return pltpu.make_async_remote_copy(
+        src_ref=src,
+        dst_ref=dst,
+        send_sem=send.at[at],
+        recv_sem=recv.at[at],
+        device_id=where,
+        device_id_type=pl.DeviceIdType.MESH,
+    )
 
 
 def group_kernel(
     owners,
-    persons,
-    per_owner,
-    trow,
-    tcol,
-    me_ref,
-    tiles,
-    match_row,
-    diag,
-    col_row,
-    col_col,
-    row_row,
-    row_col,
-    weight,
+    imeta,
+    fmeta,
+    pairs,
     pheno,
     x_out,
     r_out,
-    kb,
-    ktb,
+    imeta_all,
+    fmeta_all,
+    tiles_all,
+    ph_all,
+    inv_v,
+    inv,
+    match_row,
+    col_row,
+    row_row,
+    col_col,
+    row_col,
+    weight,
+    diag,
     khi,
     klo,
     kthi,
@@ -217,30 +205,184 @@
     rselt,
     d,
     r,
+    xs,
     dcat,
     ycat,
     hcat,
+    meta_send,
+    meta_recv,
+    tile_send,
+    tile_recv,
+    ph_send,
+    ph_recv,
+    out_send,
+    out_recv,
+    local_sem,
 ):
+    persons = pheno.shape[0]
     every = owners * persons
     entries = c.shape[0]
     eown = entries // owners
-    n = pheno.shape[1]
+    n = d.shape[1]
+    held = pairs.shape[0]
+    share = held // 2
+    half = persons // 2
     nblk = persons // 64
-    me = me_ref[0]
-
-    @pl.when(pl.program_id(0) == 0)
-    def _():
-        build_factor(
-            owners, per_owner, nblk, trow, tcol, tiles, kb, ktb, khi, klo, kthi, ktlo
+    lists = 2 * owners
+    blank = lists * held
+    f = lax.axis_index("fam")
+    t = lax.axis_index("trait")
+    rep = lax.axis_index("rep")
+    other = 1 - rep
+    across = 1 - t
+    me = f * 2 + rep
+    peers = [lax.rem(f + k, owners) for k in range(1, owners)]
+    sources = [lax.rem(f + owners - k, owners) for k in range(1, owners)]
+
+    barrier = pltpu.get_barrier_semaphore()
+    greet = [dict(fam=p, rep=q) for p in peers for q in (rep, other)]
+    greet += [dict(rep=other), dict(trait=across)]
+    for g in greet:
+        pl.semaphore_signal(barrier, inc=1, device_id=g, device_id_type=pl.DeviceIdType.MESH)
+    pl.semaphore_wait(barrier, len(greet))
+
+    meta_sems = (meta_send, meta_recv)
+    meta_copies = []
+    at = 0
+    for own, all_ in ((imeta, imeta_all), (fmeta, fmeta_all)):
+        for g in greet[:-1]:
+            cp = copy_to(own, all_.at[me], meta_sems, at, **g)
+            cp.start()
+            meta_copies.append(cp)
+            at += 1
+
+    def tiles_of(source, who, part):
+        first = (source * 2 + who) * held + part * share
+        return tiles_all.at[pl.ds(first, share)]
+
+    tile_sems = (tile_send, tile_recv)
+    k3 = owners - 1
+    along = []
+    for k, p in enumerate(peers):
+        cp = copy_to(pairs.at[pl.ds(t * share, share)], tiles_of(f, rep, t), tile_sems, k, fam=p)
+        cp.start()
+        along.append(cp)
+    own_tiles = tiles_all.at[pl.ds(me * held, held)]
+    tile_home = copy_to(pairs, own_tiles, tile_sems, 4 * k3, rep=other)
+    tile_home.start()
+
+    ph_sems = (ph_send, ph_recv)
+    ph_along = []
+    for k, p in enumerate(peers):
+        cp = copy_to(
+            pheno.at[pl.ds(rep * half, half), pl.ds(pl.multiple_of(p * n, n), n)],
+            ph_all.at[pl.ds(f * persons + rep * half, half)],
+            ph_sems,
+            k,
+            fam=p,
         )
-        one_hot_cols(pm, match_row, every, 64)
-        one_hot_rows(c, col_col, entries, 64)
-        one_hot_cols(ct, col_row, every, 64)
-        one_hot_rows(rsel, row_col, entries, 64)
-        for o in range(owners):
-            lane = row_row[:, o * eown : (o + 1) * eown]
-            sub = lax.broadcasted_iota(jnp.int32, (persons, eown), 0)
-            rselt[o] = jnp.where(lane == sub, 1.0, 0.0).astype(jnp.bfloat16)
+        cp.start()
+        ph_along.append(cp)
+
+    keep = [
+        pltpu.make_async_copy(imeta, imeta_all.at[me], local_sem.at[0]),
+        pltpu.make_async_copy(fmeta, fmeta_all.at[me], local_sem.at[1]),
+        pltpu.make_async_copy(pairs, own_tiles, local_sem.at[2]),
+        pltpu.make_async_copy(
+            pheno.at[:, pl.ds(pl.multiple_of(f * n, n), n)],
+            ph_all.at[pl.ds(f * persons, persons)],
+            local_sem.at[3],
+        ),
+    ]
+    for cp in keep:
+        cp.start()
+    tiles_all[blank] = jnp.zeros(tiles_all.shape[1:], jnp.float32)
+    for cp in keep:
+        cp.wait()
+    for cp in meta_copies:
+        cp.wait()
+
+    inv_v[...] = jnp.zeros(inv_v.shape, jnp.int32)
+    pos_lane = lax.broadcasted_iota(jnp.int32, (held, n), 1)
+    tile_id = lax.broadcasted_iota(jnp.int32, (held, n), 0)
+    for o in range(owners):
+        found = jnp.zeros((1, n), jnp.int32)
+        for q in range(2):
+            j = 2 * o + q
+            im = imeta_all[j]
+            imt = im.T
+            at = slice(j * n, (j + 1) * n)
+            col_row[:, at] = im[4:5]
+            row_row[:, at] = im[5:6]
+            col_col[at, :] = imt[:, 4:5]
+            row_col[at, :] = imt[:, 5:6]
+            fmt = fmeta_all[j].T
+            weight[at, :] = fmt[:, 4:5]
+            hit = jnp.where(imt[:held, 6:7] == pos_lane, tile_id + (j * held + 1), 0)
+            found = jnp.maximum(found, jnp.max(hit, axis=0, keepdims=True))
+            if q == 0:
+                for i in range(persons // n):
+                    at = slice(o * persons + i * n, o * persons + (i + 1) * n)
+                    match_row[:, at] = im[i : i + 1]
+                    diag[at, :] = fmt[:, i : i + 1]
+        inv_v[o : o + 1, :] = jnp.where(found == 0, blank, found - 1)
+    to_scalar = pltpu.make_async_copy(inv_v, inv, local_sem.at[4])
+    to_scalar.start()
+
+    one_hot_rows(c, col_col, entries, 64)
+    one_hot_cols(ct, col_row, every, 64)
+    tile_across, tile_side = [], []
+    for k, s in enumerate(sources):
+        along[k].wait()
+        cp = copy_to(tiles_of(s, rep, t), tiles_of(s, rep, t), tile_sems, k3 + k, trait=across)
+        cp.start()
+        tile_across.append(cp)
+        cp = copy_to(tiles_of(s, rep, t), tiles_of(s, rep, t), tile_sems, 2 * k3 + k, rep=other)
+        cp.start()
+        tile_side.append(cp)
+    one_hot_rows(rsel, row_col, entries, 64)
+    for o in range(owners):
+        lane = row_row[:, o * eown : (o + 1) * eown]
+        sub = lax.broadcasted_iota(jnp.int32, (persons, eown), 0)
+        rselt[o] = jnp.where(lane == sub, 1.0, 0.0).astype(jnp.bfloat16)
+    for k, s in enumerate(sources):
+        tile_across[k].wait()
+        part = tiles_of(s, rep, across)
+        cp = copy_to(part, part, tile_sems, 3 * k3 + k, rep=other)
+        cp.start()
+        tile_side.append(cp)
+    one_hot_cols(pm, match_row, every, 64)
+    ph_side = []
+    for k, s in enumerate(sources):
+        ph_along[k].wait()
+        part = ph_all.at[pl.ds(s * persons + rep * half, half)]
+        cp = copy_to(part, part, ph_sems, k3 + k, rep=other)
+        cp.start()
+        ph_side.append(cp)
+    to_scalar.wait()
+    tile_home.wait()
+    for cp in tile_side:
+        cp.wait()
+
+    def factor(o, _):
+        for a2 in range(nblk // 2):
+            rows = []
+            for a in (2 * a2, 2 * a2 + 1):
+                got = [tiles_all[inv[o, a * nblk + b]] for b in range(nblk)]
+                rows.append(jnp.concatenate([g[:, :64] for g in got], axis=1))
+                rows.append(jnp.concatenate([g[:, 64:] for g in got], axis=1))
+            full = jnp.concatenate(rows, axis=0)
+            at = slice(a2 * 128, (a2 + 1) * 128)
+            high = full.astype(jnp.bfloat16)
+            khi[o, at, :] = high
+            klo[o, at, :] = (full - high.astype(jnp.float32)).astype(jnp.bfloat16)
+            full = full.T
+            high = full.astype(jnp.bfloat16)
+            kthi[o, :, at] = high
+            ktlo[o, :, at] = (full - high.astype(jnp.float32)).astype(jnp.bfloat16)
+        return 0
+
+    lax.fori_loop(0, owners, factor, 0)
 
     def person(o):
         return pl.ds(pl.multiple_of(o * persons, persons), persons)
@@ -253,15 +395,17 @@
     def colsum(v):
         return jnp.sum(v, axis=0, keepdims=True)
 
-    ycat[...] = split_terms(pheno[...])
+    for cp in ph_side:
+        cp.wait()
+    ycat[...] = split_terms(ph_all[...])
 
     def begin(o, carry):
         rr, dd = carry
-        t = fold(mm(pm[person(o), :], ycat[...]))
-        r[person(o), :] = t
-        d[person(o), :] = t
-        dcat[person(o), :] = split_terms(t)
-        square = t * t
+        v = fold(mm(pm[person(o), :], ycat[...]))
+        r[person(o), :] = v
+        d[person(o), :] = v
+        dcat[person(o), :] = split_terms(v)
+        square = v * v
         return rr + colsum(square), dd + colsum(square * diag[person(o), :])
 
     rr, dd = lax.fori_loop(0, owners, begin, (zero, zero))
@@ -283,17 +427,18 @@
         back = back + mm(ktlo[o], ys[:, :n])
         return diag[person(o), :] * d[person(o), :] + back
 
-    for step in range(ITERS):
+    def advance(alpha, first):
+        def body(o, _):
+            move = alpha * d[person(o), :]
+            xs[person(o), :] = move if first else xs[person(o), :] + move
+            return 0
+
+        lax.fori_loop(0, owners, body, 0)
+
+    for step in range(ITERS - 1):
         yy = lax.fori_loop(0, owners, forward, zero)
         alpha = rr / (yy + dd)
-        move = alpha * d[person(me), :]
-        if step == 0:
-            x_out[...] = move
-        else:
-            x_out[...] = x_out[...] + move
-        if step == ITERS - 1:
-            r_out[...] = r[person(me), :] - alpha * image(me)
-            break
+        advance(alpha, step == 0)
 
         def descend(o, acc):
             left = r[person(o), :] - alpha * image(o)
@@ -311,6 +456,48 @@
             return acc + colsum(v * v * diag[person(o), :])
 
         dd = lax.fori_loop(0, owners, turn, zero)
+
+    yy = lax.fori_loop(0, owners, forward, zero)
+    alpha = rr / (yy + dd)
+    advance(alpha, False)
+
+    out_sems = (out_send, out_recv)
+    mycols = pl.ds(pl.multiple_of(f * n, n), n)
+
+    def give(src, dst, k, at):
+        cp = copy_to(
+            src.at[pl.ds(peers[k] * persons + rep * half, half)],
+            dst.at[pl.ds(rep * half, half), mycols],
+            out_sems,
+            at,
+            fam=peers[k],
+        )
+        cp.start()
+        return cp
+
+    out_along = [give(xs, x_out, k, k) for k in range(k3)]
+    stay = [pltpu.make_async_copy(xs.at[pl.ds(f * persons, persons)], x_out.at[:, mycols], local_sem.at[5])]
+    stay[0].start()
+    for k in range(owners):
+        o = peers[k] if k < k3 else f
+        r[person(o), :] = r[person(o), :] - alpha * image(o)
+        if k < k3:
+            out_along.append(give(r, r_out, k, k3 + k))
+    stay.append(
+        pltpu.make_async_copy(r.at[pl.ds(f * persons, persons)], r_out.at[:, mycols], local_sem.at[6])
+    )
+    stay[1].start()
+    out_side = []
+    for i, cp in enumerate(out_along):
+        cp.wait()
+        dst = x_out if i < k3 else r_out
+        s = sources[i % k3]
+        part = dst.at[pl.ds(rep * half, half), pl.ds(pl.multiple_of(s * n, n), n)]
+        side = copy_to(part, part, out_sems, 2 * k3 + i, rep=other)
+        side.start()
+        out_side.append(side)
+    for cp in out_side + stay:
+        cp.wait()
 
 
 def local_group(
@@ -326,54 +513,44 @@
     rel_weight,
 ):
     owners = lax.axis_size("fam")
-    reps = lax.axis_size("rep")
-    traits = lax.axis_size("trait")
     persons, columns = pheno.shape
-    mine = columns // reps
-    n = 128
-    me = lax.axis_index("fam")
-    rep = lax.axis_index("rep")
+    n = columns // owners
     held = tiles.shape[0]
-    share = held // traits
+    nblk = persons // 64
     pairs = tiles.reshape(held, 32, 128)
-    pairs = lax.dynamic_slice_in_dim(pairs, lax.axis_index("trait") * share, share, 0)
-    pairs = lax.all_gather(pairs, ("fam", "rep", "trait"), tiled=True)
-    col = rel_peer[:, 0] * persons + rel_slot
     inner = rel_row % 64
     row = rel_row - inner + (inner % 2) * 32 + inner // 2
-    ints = (match, tile_row_family, tile_cols, col, row)
-    packed = jnp.concatenate([v.astype(jnp.float32) for v in ints] + [diag_var, rel_weight])
-    everyone = lax.all_gather(packed, ("fam", "rep")).reshape(owners, reps, -1)
-    sizes = [v.shape[0] for v in ints] + [persons, rel_row.shape[0]]
-    parts, at = [], 0
-    for size in sizes:
-        parts.append(everyone[:, :, at : at + size])
-        at += size
-    match_all = parts[0][:, 0].reshape(1, -1).astype(jnp.int32)
-    trow = parts[1].reshape(-1).astype(jnp.int32)
-    tcol = parts[2].reshape(-1).astype(jnp.int32)
-    col_all = parts[3].reshape(-1).astype(jnp.int32)
-    row_all = parts[4].reshape(-1).astype(jnp.int32)
-    diag_all = parts[5][:, 0].reshape(-1, 1)
-    weight_all = parts[6].reshape(-1, 1)
-    part = lax.dynamic_slice_in_dim(pheno, rep * mine, mine, 1)
-    gathered = lax.all_gather(part, "fam", tiled=True)
+    col = rel_peer[:, 0] * persons + rel_slot
+    place = jnp.pad(tile_row_family * nblk + tile_cols, (0, n - held), constant_values=-1)
+    imeta = jnp.concatenate([match, col, row, place, place]).reshape(8, n)
+    fmeta = jnp.concatenate([diag_var, rel_weight, rel_weight, rel_weight, rel_weight]).reshape(8, n)
+    lists = 2 * owners
     every = owners * persons
-    entries = col_all.shape[0]
+    entries = lists * rel_row.shape[0]
     eown = entries // owners
-    nblk = persons // 64
-    smem = pl.BlockSpec(memory_space=pltpu.SMEM)
     vmem = pl.BlockSpec(memory_space=pltpu.VMEM)
-    bf = jnp.bfloat16
-    x, r = pl.pallas_call(
-        functools.partial(group_kernel, owners, persons, held * reps),
-        grid=(mine // n,),
-        out_shape=[jax.ShapeDtypeStruct((persons, mine), jnp.float32)] * 2,
-        in_specs=[smem] * 3 + [vmem] * 8 + [pl.BlockSpec((every, n), lambda i: (0, i))],
-        out_specs=[pl.BlockSpec((persons, n), lambda i: (0, i))] * 2,
+    bf, f32, i32 = jnp.bfloat16, jnp.float32, jnp.int32
+    k3 = owners - 1
+    dma = pltpu.SemaphoreType.DMA
+    return pl.pallas_call(
+        functools.partial(group_kernel, owners),
+        out_shape=[jax.ShapeDtypeStruct((persons, columns), f32)] * 2,
+        in_specs=[vmem] * 4,
+        out_specs=[vmem] * 2,
         scratch_shapes=[
-            pltpu.VMEM((nblk, persons, 64), jnp.float32),
-            pltpu.VMEM((nblk, persons, 64), jnp.float32),
+            pltpu.VMEM((lists, 8, n), i32),
+            pltpu.VMEM((lists, 8, n), f32),
+            pltpu.VMEM((lists * held + 1, 32, 128), f32),
+            pltpu.VMEM((every, n), f32),
+            pltpu.VMEM((8, n), i32),
+            pltpu.SMEM((8, n), i32),
+            pltpu.VMEM((1, every), i32),
+            pltpu.VMEM((1, entries), i32),
+            pltpu.VMEM((1, entries), i32),
+            pltpu.VMEM((entries, 1), i32),
+            pltpu.VMEM((entries, 1), i32),
+            pltpu.VMEM((entries, 1), f32),
+            pltpu.VMEM((every, 1), f32),
             pltpu.VMEM((owners, persons, persons), bf),
             pltpu.VMEM((owners, persons, persons), bf),
             pltpu.VMEM((owners, persons, persons), bf),
@@ -383,30 +560,26 @@
             pltpu.VMEM((every, entries), bf),
             pltpu.VMEM((entries, persons), bf),
             pltpu.VMEM((owners, persons, eown), bf),
-            pltpu.VMEM((every, n), jnp.float32),
-            pltpu.VMEM((every, n), jnp.float32),
+            pltpu.VMEM((every, n), f32),
+            pltpu.VMEM((every, n), f32),
+            pltpu.VMEM((every, n), f32),
             pltpu.VMEM((every, 2 * n), bf),
             pltpu.VMEM((every, 2 * n), bf),
             pltpu.VMEM((entries, 2 * n), bf),
+            dma((2 * lists - 2,)),
+            dma((2 * lists - 2,)),
+            dma((4 * k3 + 1,)),
+            dma((4 * k3 + 1,)),
+            dma((2 * k3,)),
+            dma((2 * k3,)),
+            dma((4 * k3,)),
+            dma((4 * k3,)),
+            dma((7,)),
         ],
-        compiler_params=pltpu.CompilerParams(vmem_limit_bytes=60 * 2**20),
-    )(
-        trow,
-        tcol,
-        me.reshape(1),
-        pairs,
-        match_all,
-        diag_all,
-        col_all.reshape(1, -1),
-        col_all.reshape(-1, 1),
-        row_all.reshape(1, -1),
-        row_all.reshape(-1, 1),
-        weight_all,
-        gathered,
-    )
-    x = lax.all_gather(x, "rep", axis=1, tiled=True)
-    r = lax.all_gather(r, "rep", axis=1, tiled=True)
-    return x, r
+        compiler_params=pltpu.CompilerParams(
+            vmem_limit_bytes=60 * 2**20, collective_id=0, has_side_effects=True
+        ),
+    )(imeta, fmeta, pairs, pheno)
 
 
 def solution(mesh):
@@ -422,7 +595,7 @@
         P(("groups", "fam", "rep")),
         P(("groups", "fam", "rep")),
     )
-    whole = mesh.shape["fam"] <= 4
+    whole = mesh.shape["fam"] == 4 and mesh.shape["trait"] == 2 and mesh.shape["rep"] == 2
     return jax.shard_map(
         local_group if whole else local,
         mesh=mesh,

time: 221 us -> 99.5 us (0.45)
  waiting for transfers between devices: 73.5 us -> 0 us
  blocking collectives: 27.3 us -> 0 us
  between operations: 14.6 us -> 0.74 us
  local copies, waits for them, and re-layouts: 13.8 us -> 9.05 us
    all_gather x4 -> x0, waiting for transfers between devices: 72.9 us -> none  [the longest x1 43.8 us: local_group(): pairs = lax.all_gather(pairs, ('fam', 'rep', 'trait'), tiled=True)]
    unnamed x1 -> x0, blocking collectives: 27.3 us -> none
    convert_element_type x4 -> x0, local copies, waits for them, and re-layouts: 3.35 us -> none  [the longest x1 1.03 us: local_group(): row_all = parts[4].reshape(-1).astype(jnp.int32)]
    unnamed x32 -> x31, local copies, waits for them, and re-layouts: 6.42 us -> 9.04 us
  transfers between devices with their start and end apart: 4 -> 0, of which waited for: 4 -> 0; matrix products, arithmetic and copies ran while one was open for 4% -> 0% of each run, Pallas kernels for 0% -> 0%
where the time goes in v2:
time: 99.5 us; the launch traced here: 99.2 us
  Pallas kernels  89.4 us (90%)
  local copies, waits for them, and re-layouts  9.05 us (9%)
    pallas_call x1, Pallas kernels, local_group(): pl.pallas_call(functools.partial(group_kernel, owners), out_shape=[jax.Sh...  89.4 us
    unnamed x31, local copies, waits for them, and re-layouts  9.04 us

profile of v2, /device:TPU:25, one launch (start us, length us, event | category | flops | bytes accessed | tf_op | source)
XLA Modules:
  0.0 99.2 jit_solution(700643073224060096)
XLA Ops:
  0.6 0.0 copy-start.5
  0.6 0.0 copy-start.6
  0.7 0.6 copy-done.5
  1.3 0.0 copy-done.6
  1.3 0.0 copy-start.3
  1.3 0.7 copy-done.3
  2.0 0.0 copy-start.7
  2.0 0.6 copy-done.7
  2.6 0.0 copy-done.8
  2.7 0.0 copy-start.9
  2.7 0.6 copy-done.9
  3.4 0.0 copy-start.1
  3.4 0.0 copy-start.4
  3.4 0.7 copy-done.4
  4.1 0.6 copy-done.10
  4.7 0.0 copy-done.1
  4.8 0.0 copy-start.2
  4.8 1.7 %copy.12 = f32[2,8,32,128]{3,2,1,0:T(8,128)} copy(f32[2,8,32,128]{3,1,2,0:T(8,128)} %bitcast.9) | data formatting | bytes 524288
  6.5 0.0 copy-done.2
  6.5 89.4 %shard_map.113 = (f32[512,512]{1,0:T(8,128)}, f32[512,512]{1,0:T(8,128)}) custom-call(s32[8,128]{1,0:T(8,128)} %bitcast.10, f32[8,128]{1,0:T(8,128)} %bitcast.11, f32[16,32,128]{2,1,0:T(8,128)} %bitcast.8, f32[512,512]{1,0:T(8,128)} %pheno.1), custom_call_target="tpu_custom_call" | custom-call | tf_op jit(solution)/shard_map/pallas_call | solution.py:535
  95.9 0.0 copy-start
  95.9 2.4 %copy.25 = f32[512,512]{1,0:T(8,128)} copy(f32[512,512]{1,0:T(8,128)} %get-tuple-element.4) | data formatting | bytes 2097152
  98.2 0.0 copy-done
  98.2 1.0 copy.26
  (15 shorter events, 0.1 us)
Async XLA Ops:
  0.6 0.7 copy-start.5
  0.6 0.7 copy-start.6
  1.3 0.7 copy-start.3
  2.0 0.7 copy-start.7
  2.0 0.7 copy-start.8
  2.7 0.7 copy-start.9
  3.4 1.4 %copy-start.1 = (s32[1024]{0:T(1024)}, s32[1024]{0:T(1024)S(1)}, u32[]{:S(2)}) copy-start(s32[1024]{0:T(1024)S(1)} %constant_dynamic-update-slice_fusion) | copy-start | bytes 12292
  3.4 0.7 copy-start.4
  4.1 0.7 copy-start.10
  4.8 1.7 %copy-start.2 = (f32[1024]{0:T(1024)}, f32[1024]{0:T(1024)S(1)}, u32[]{:S(2)}) copy-start(f32[1024]{0:T(1024)S(1)} %constant_dynamic-update-slice_fusion.1) | copy-start | bytes 12292
  95.9 2.4 %copy-start = (f32[512,512]{1,0:T(8,128)S(1)}, f32[512,512]{1,0:T(8,128)}, u32[]{:S(2)}) copy-start(f32[512,512]{1,0:T(8,128)} %get-tuple-element.5) | copy-start | bytes 3145732

commit v3 on v2

--- a/solution.py
+++ b/solution.py
@@ -175,12 +175,21 @@
 
 def group_kernel(
     owners,
+    match,
+    diag_own,
+    tiles,
+    trow,
+    tcol,
+    rel_row,
+    rel_peer,
+    rel_slot,
+    rel_weight,
+    pheno,
+    x_out,
+    r_out,
     imeta,
     fmeta,
     pairs,
-    pheno,
-    x_out,
-    r_out,
     imeta_all,
     fmeta_all,
     tiles_all,
@@ -205,7 +214,9 @@
     rselt,
     d,
     r,
-    xs,
+    got,
+    al,
+    al_all,
     dcat,
     ycat,
     hcat,
@@ -217,13 +228,14 @@
     ph_recv,
     out_send,
     out_recv,
+    relay_send,
     local_sem,
 ):
     persons = pheno.shape[0]
     every = owners * persons
     entries = c.shape[0]
     eown = entries // owners
-    n = d.shape[1]
+    n = r.shape[1]
     held = pairs.shape[0]
     share = held // 2
     half = persons // 2
@@ -244,6 +256,18 @@
     greet += [dict(rep=other), dict(trait=across)]
     for g in greet:
         pl.semaphore_signal(barrier, inc=1, device_id=g, device_id_type=pl.DeviceIdType.MESH)
+
+    inner = rel_row[...] % 64
+    imeta[...] = jnp.full(imeta.shape, -1, jnp.int32)
+    fmeta[...] = jnp.zeros(fmeta.shape, jnp.float32)
+    imeta[0 : persons // n, :] = match[...]
+    imeta[4:5, :] = rel_peer[...] * persons + rel_slot[...]
+    imeta[5:6, :] = rel_row[...] - inner + (inner % 2) * 32 + inner // 2
+    imeta[6:7, 0:held] = trow[...] * nblk + tcol[...]
+    fmeta[0 : persons // n, :] = diag_own[...]
+    fmeta[4:5, :] = rel_weight[...]
+    for i in range(32):
+        pairs[:, i, :] = tiles[:, i * 128 : (i + 1) * 128]
     pl.semaphore_wait(barrier, len(greet))
 
     meta_sems = (meta_send, meta_recv)
@@ -262,11 +286,37 @@
 
     tile_sems = (tile_send, tile_recv)
     k3 = owners - 1
-    along = []
-    for k, p in enumerate(peers):
-        cp = copy_to(pairs.at[pl.ds(t * share, share)], tiles_of(f, rep, t), tile_sems, k, fam=p)
-        cp.start()
-        along.append(cp)
+    near = f + 1 - 2 * lax.rem(f, 2)
+    is_inner = (f == 1) | (f == 2)
+    partner = 3 - f
+    origin = [near, jnp.where(is_inner, partner, 3 - near), jnp.where(is_inner, 3 - near, partner)]
+    own_share = pairs.at[pl.ds(t * share, share)]
+    to_near = copy_to(own_share, tiles_of(f, rep, t), tile_sems, 0, fam=near)
+    to_near.start()
+
+    def relay(src, owner, send_at, recv_at, to):
+        cp = pltpu.make_async_remote_copy(
+            src_ref=src,
+            dst_ref=tiles_of(owner, rep, t),
+            send_sem=relay_send.at[send_at],
+            recv_sem=tile_recv.at[recv_at],
+            device_id=dict(fam=to),
+            device_id_type=pl.DeviceIdType.MESH,
+        )
+        return cp
+
+    across_mid = jnp.where(is_inner, partner, near)
+    relays = [
+        relay(own_share, f, 0, 1, across_mid),
+        relay(tiles_of(origin[0], rep, t), origin[0], 1, 2, across_mid),
+        relay(tiles_of(origin[1], rep, t), origin[1], 2, 1, near),
+        relay(tiles_of(origin[2], rep, t), origin[2], 3, 2, near),
+    ]
+
+    @pl.when(is_inner)
+    def _():
+        relays[0].start()
+
     own_tiles = tiles_all.at[pl.ds(me * held, held)]
     tile_home = copy_to(pairs, own_tiles, tile_sems, 4 * k3, rep=other)
     tile_home.start()
@@ -332,8 +382,16 @@
     one_hot_rows(c, col_col, entries, 64)
     one_hot_cols(ct, col_row, every, 64)
     tile_across, tile_side = [], []
-    for k, s in enumerate(sources):
-        along[k].wait()
+    for k, s in enumerate(origin):
+        if k == 0:
+            to_near.wait()
+        else:
+            copy_to(own_share, tiles_of(s, rep, t), tile_sems, k, fam=near).wait_recv()
+
+        @pl.when(is_inner)
+        def _():
+            relays[k + 1].start()
+
         cp = copy_to(tiles_of(s, rep, t), tiles_of(s, rep, t), tile_sems, k3 + k, trait=across)
         cp.start()
         tile_across.append(cp)
@@ -345,24 +403,23 @@
         lane = row_row[:, o * eown : (o + 1) * eown]
         sub = lax.broadcasted_iota(jnp.int32, (persons, eown), 0)
         rselt[o] = jnp.where(lane == sub, 1.0, 0.0).astype(jnp.bfloat16)
-    for k, s in enumerate(sources):
+    for k, s in enumerate(origin):
         tile_across[k].wait()
         part = tiles_of(s, rep, across)
         cp = copy_to(part, part, tile_sems, 3 * k3 + k, rep=other)
         cp.start()
         tile_side.append(cp)
     one_hot_cols(pm, match_row, every, 64)
-    ph_side = []
-    for k, s in enumerate(sources):
-        ph_along[k].wait()
-        part = ph_all.at[pl.ds(s * persons + rep * half, half)]
-        cp = copy_to(part, part, ph_sems, k3 + k, rep=other)
-        cp.start()
-        ph_side.append(cp)
     to_scalar.wait()
     tile_home.wait()
     for cp in tile_side:
         cp.wait()
+
+    @pl.when(is_inner)
+    def _():
+        for cp in relays:
+            cp.wait_send()
+
 
     def factor(o, _):
         for a2 in range(nblk // 2):
@@ -384,6 +441,14 @@
 
     lax.fori_loop(0, owners, factor, 0)
 
+    ph_side = []
+    for k, s in enumerate(sources):
+        ph_along[k].wait()
+        part = ph_all.at[pl.ds(s * persons + rep * half, half)]
+        cp = copy_to(part, part, ph_sems, k3 + k, rep=other)
+        cp.start()
+        ph_side.append(cp)
+
     def person(o):
         return pl.ds(pl.multiple_of(o * persons, persons), persons)
 
@@ -398,17 +463,31 @@
     for cp in ph_side:
         cp.wait()
     ycat[...] = split_terms(ph_all[...])
+
+    out_sems = (out_send, out_recv)
+
+    def block(o):
+        return pl.ds(pl.multiple_of(o * n, n), n)
+
+    def give(src, dst, k, at):
+        cp = copy_to(src.at[pl.ds(peers[k] * persons + rep * half, half)], dst, out_sems, at, fam=peers[k])
+        cp.start()
+        return cp
+
+    def give_direction(step):
+        return [give(d.at[step], got.at[step, :, block(f)], k, step * k3 + k) for k in range(k3)]
 
     def begin(o, carry):
         rr, dd = carry
         v = fold(mm(pm[person(o), :], ycat[...]))
         r[person(o), :] = v
-        d[person(o), :] = v
+        d[0, person(o), :] = v
         dcat[person(o), :] = split_terms(v)
         square = v * v
         return rr + colsum(square), dd + colsum(square * diag[person(o), :])
 
     rr, dd = lax.fori_loop(0, owners, begin, (zero, zero))
+    given = give_direction(0)
 
     def forward(o, yy):
         g = fold(mm(c[entry(o), :], dcat[...])) * weight[entry(o), :]
@@ -421,27 +500,19 @@
         hcat[entry(o), :] = split_terms(h)
         return yy + colsum(y * y)
 
-    def image(o):
+    def image(o, step):
         ys = ycat[person(o), :]
         back = fold(mm(kthi[o], ys) + mm(ct[person(o), :], hcat[...]))
         back = back + mm(ktlo[o], ys[:, :n])
-        return diag[person(o), :] * d[person(o), :] + back
-
-    def advance(alpha, first):
-        def body(o, _):
-            move = alpha * d[person(o), :]
-            xs[person(o), :] = move if first else xs[person(o), :] + move
-            return 0
-
-        lax.fori_loop(0, owners, body, 0)
+        return diag[person(o), :] * d[step, person(o), :] + back
 
     for step in range(ITERS - 1):
         yy = lax.fori_loop(0, owners, forward, zero)
         alpha = rr / (yy + dd)
-        advance(alpha, step == 0)
+        al[step : step + 1, :] = alpha
 
         def descend(o, acc):
-            left = r[person(o), :] - alpha * image(o)
+            left = r[person(o), :] - alpha * image(o, step)
             r[person(o), :] = left
             return acc + colsum(left * left)
 
@@ -450,53 +521,58 @@
         rr = nxt
 
         def turn(o, acc):
-            v = r[person(o), :] + beta * d[person(o), :]
-            d[person(o), :] = v
+            v = r[person(o), :] + beta * d[step, person(o), :]
+            d[step + 1, person(o), :] = v
             dcat[person(o), :] = split_terms(v)
             return acc + colsum(v * v * diag[person(o), :])
 
         dd = lax.fori_loop(0, owners, turn, zero)
-
+        given += give_direction(step + 1)
+
+    last = ITERS - 1
     yy = lax.fori_loop(0, owners, forward, zero)
     alpha = rr / (yy + dd)
-    advance(alpha, False)
-
-    out_sems = (out_send, out_recv)
-    mycols = pl.ds(pl.multiple_of(f * n, n), n)
-
-    def give(src, dst, k, at):
-        cp = copy_to(
-            src.at[pl.ds(peers[k] * persons + rep * half, half)],
-            dst.at[pl.ds(rep * half, half), mycols],
-            out_sems,
-            at,
-            fam=peers[k],
-        )
-        cp.start()
-        return cp
-
-    out_along = [give(xs, x_out, k, k) for k in range(k3)]
-    stay = [pltpu.make_async_copy(xs.at[pl.ds(f * persons, persons)], x_out.at[:, mycols], local_sem.at[5])]
-    stay[0].start()
+    al[last : last + 1, :] = alpha
+    base = ITERS * k3
+    told = []
+    for k in range(k3):
+        cp = copy_to(al, al_all.at[f], out_sems, base + k, fam=peers[k])
+        cp.start()
+        told.append(cp)
+
+    mine = pl.ds(rep * half, half)
+    theirs = []
     for k in range(owners):
         o = peers[k] if k < k3 else f
-        r[person(o), :] = r[person(o), :] - alpha * image(o)
+        r[person(o), :] = r[person(o), :] - alpha * image(o, last)
         if k < k3:
-            out_along.append(give(r, r_out, k, k3 + k))
-    stay.append(
-        pltpu.make_async_copy(r.at[pl.ds(f * persons, persons)], r_out.at[:, mycols], local_sem.at[6])
-    )
-    stay[1].start()
-    out_side = []
-    for i, cp in enumerate(out_along):
+            theirs.append(give(r, r_out.at[mine, block(f)], k, base + k3 + k))
+    stay = pltpu.make_async_copy(
+        r.at[pl.ds(f * persons, persons)], r_out.at[:, block(f)], local_sem.at[5]
+    )
+    stay.start()
+    for cp in given + told:
         cp.wait()
-        dst = x_out if i < k3 else r_out
-        s = sources[i % k3]
-        part = dst.at[pl.ds(rep * half, half), pl.ds(pl.multiple_of(s * n, n), n)]
-        side = copy_to(part, part, out_sems, 2 * k3 + i, rep=other)
-        side.start()
-        out_side.append(side)
-    for cp in out_side + stay:
+
+    home = pl.ds(f * persons + rep * half, half)
+    total = al[0:1, :] * d[0, home, :]
+    for u in range(1, ITERS):
+        total = total + al[u : u + 1, :] * d[u, home, :]
+    x_out[mine, block(f)] = total
+    for s in sources:
+        total = al_all[s, 0:1, :] * got[0, :, block(s)]
+        for u in range(1, ITERS):
+            total = total + al_all[s, u : u + 1, :] * got[u, :, block(s)]
+        x_out[mine, block(s)] = total
+    side = [copy_to(x_out.at[mine], x_out.at[mine], out_sems, base + 2 * k3, rep=other)]
+    side[0].start()
+    for i, cp in enumerate(theirs):
+        cp.wait()
+        part = r_out.at[mine, block(sources[i])]
+        cp = copy_to(part, part, out_sems, base + 2 * k3 + 1 + i, rep=other)
+        cp.start()
+        side.append(cp)
+    for cp in side + [stay]:
         cp.wait()
 
 
@@ -516,14 +592,6 @@
     persons, columns = pheno.shape
     n = columns // owners
     held = tiles.shape[0]
-    nblk = persons // 64
-    pairs = tiles.reshape(held, 32, 128)
-    inner = rel_row % 64
-    row = rel_row - inner + (inner % 2) * 32 + inner // 2
-    col = rel_peer[:, 0] * persons + rel_slot
-    place = jnp.pad(tile_row_family * nblk + tile_cols, (0, n - held), constant_values=-1)
-    imeta = jnp.concatenate([match, col, row, place, place]).reshape(8, n)
-    fmeta = jnp.concatenate([diag_var, rel_weight, rel_weight, rel_weight, rel_weight]).reshape(8, n)
     lists = 2 * owners
     every = owners * persons
     entries = lists * rel_row.shape[0]
@@ -535,9 +603,12 @@
     return pl.pallas_call(
         functools.partial(group_kernel, owners),
         out_shape=[jax.ShapeDtypeStruct((persons, columns), f32)] * 2,
-        in_specs=[vmem] * 4,
+        in_specs=[vmem] * 10,
         out_specs=[vmem] * 2,
         scratch_shapes=[
+            pltpu.VMEM((8, n), i32),
+            pltpu.VMEM((8, n), f32),
+            pltpu.VMEM((held, 32, 128), f32),
             pltpu.VMEM((lists, 8, n), i32),
             pltpu.VMEM((lists, 8, n), f32),
             pltpu.VMEM((lists * held + 1, 32, 128), f32),
@@ -560,9 +631,11 @@
             pltpu.VMEM((every, entries), bf),
             pltpu.VMEM((entries, persons), bf),
             pltpu.VMEM((owners, persons, eown), bf),
+            pltpu.VMEM((ITERS, every, n), f32),
             pltpu.VMEM((every, n), f32),
-            pltpu.VMEM((every, n), f32),
-            pltpu.VMEM((every, n), f32),
+            pltpu.VMEM((ITERS, persons // 2, columns), f32),
+            pltpu.VMEM((8, n), f32),
+            pltpu.VMEM((owners, 8, n), f32),
             pltpu.VMEM((every, 2 * n), bf),
             pltpu.VMEM((every, 2 * n), bf),
             pltpu.VMEM((entries, 2 * n), bf),
@@ -572,14 +645,26 @@
             dma((4 * k3 + 1,)),
             dma((2 * k3,)),
             dma((2 * k3,)),
-            dma((4 * k3,)),
-            dma((4 * k3,)),
+            dma(((ITERS + 3) * k3 + 1,)),
+            dma(((ITERS + 3) * k3 + 1,)),
+            dma((4,)),
             dma((7,)),
         ],
         compiler_params=pltpu.CompilerParams(
             vmem_limit_bytes=60 * 2**20, collective_id=0, has_side_effects=True
         ),
-    )(imeta, fmeta, pairs, pheno)
+    )(
+        match.reshape(-1, n),
+        diag_var.reshape(-1, n),
+        tiles,
+        tile_row_family.reshape(1, -1),
+        tile_cols.reshape(1, -1),
+        rel_row.reshape(1, -1),
+        rel_peer.reshape(1, -1),
+        rel_slot.reshape(1, -1),
+        rel_weight.reshape(1, -1),
+        pheno,
+    )
 
 
 def solution(mesh):

time: 99.5 us -> 93.9 us (0.944)
  local copies, waits for them, and re-layouts: 9.05 us -> 3.32 us
    unnamed x31 -> x4, local copies, waits for them, and re-layouts: 9.04 us -> 3.32 us
where the time goes in v3:
time: 93.9 us; the launch traced here: 93.8 us
  Pallas kernels  89.8 us (96%)
  local copies, waits for them, and re-layouts  3.32 us (4%)
    pallas_call x1, Pallas kernels, local_group(): pl.pallas_call(functools.partial(group_kernel, owners), out_shape=[jax.Sh...  89.8 us
    unnamed x4, local copies, waits for them, and re-layouts  3.32 us

profile of v3, /device:TPU:25, one launch (start us, length us, event | category | flops | bytes accessed | tf_op | source)
XLA Modules:
  0.0 93.8 jit_solution(1978916647761645155)
XLA Ops:
  0.6 89.8 %shard_map.113 = (f32[512,512]{1,0:T(8,128)}, f32[512,512]{1,0:T(8,128)}) custom-call(s32[4,128]{1,0:T(4,128)} %bitcast.8, f32[4,128]{1,0:T(4,128)} %bitcast.9, f32[16,4096]{1,0:T(8,128)} %tiles.1, s32[1,16]{1,0:T(1,128)} %bitcast.10, s32[1,16]{1,0:T(1,128)} %bitcast.11, s32[1,128]{1,0:T(1,128)} %bitcast.12, s32[1,128]{1,0:T(1,128)} %bitcast.13, ...), custom_call_target="tpu_custom_call" | custom-call | tf_op jit(solution)/shard_map/pallas_call | solution.py:603
  90.4 0.0 copy-start
  90.4 2.4 %copy.14 = f32[512,512]{1,0:T(8,128)} copy(f32[512,512]{1,0:T(8,128)} %get-tuple-element.4) | data formatting | bytes 2097152
  92.8 0.0 copy-done
  92.8 1.0 %copy.15 = f32[512,512]{1,0:T(8,128)} copy(f32[512,512]{1,0:T(8,128)S(1)} %copy-done) | data formatting | bytes 2097152
Async XLA Ops:
  90.4 2.4 %copy-start = (f32[512,512]{1,0:T(8,128)S(1)}, f32[512,512]{1,0:T(8,128)}, u32[]{:S(2)}) copy-start(f32[512,512]{1,0:T(8,128)} %get-tuple-element.5) | copy-start | bytes 3145732

commit v4 on v3

--- a/solution.py
+++ b/solution.py
@@ -214,6 +214,7 @@
     rselt,
     d,
     r,
+    xs,
     got,
     al,
     al_all,
@@ -228,7 +229,6 @@
     ph_recv,
     out_send,
     out_recv,
-    relay_send,
     local_sem,
 ):
     persons = pheno.shape[0]
@@ -286,53 +286,14 @@
 
     tile_sems = (tile_send, tile_recv)
     k3 = owners - 1
-    near = f + 1 - 2 * lax.rem(f, 2)
-    is_inner = (f == 1) | (f == 2)
-    partner = 3 - f
-    origin = [near, jnp.where(is_inner, partner, 3 - near), jnp.where(is_inner, 3 - near, partner)]
-    own_share = pairs.at[pl.ds(t * share, share)]
-    to_near = copy_to(own_share, tiles_of(f, rep, t), tile_sems, 0, fam=near)
-    to_near.start()
-
-    def relay(src, owner, send_at, recv_at, to):
-        cp = pltpu.make_async_remote_copy(
-            src_ref=src,
-            dst_ref=tiles_of(owner, rep, t),
-            send_sem=relay_send.at[send_at],
-            recv_sem=tile_recv.at[recv_at],
-            device_id=dict(fam=to),
-            device_id_type=pl.DeviceIdType.MESH,
-        )
-        return cp
-
-    across_mid = jnp.where(is_inner, partner, near)
-    relays = [
-        relay(own_share, f, 0, 1, across_mid),
-        relay(tiles_of(origin[0], rep, t), origin[0], 1, 2, across_mid),
-        relay(tiles_of(origin[1], rep, t), origin[1], 2, 1, near),
-        relay(tiles_of(origin[2], rep, t), origin[2], 3, 2, near),
-    ]
-
-    @pl.when(is_inner)
-    def _():
-        relays[0].start()
-
+    along = []
+    for k, p in enumerate(peers):
+        cp = copy_to(pairs.at[pl.ds(t * share, share)], tiles_of(f, rep, t), tile_sems, k, fam=p)
+        cp.start()
+        along.append(cp)
     own_tiles = tiles_all.at[pl.ds(me * held, held)]
     tile_home = copy_to(pairs, own_tiles, tile_sems, 4 * k3, rep=other)
     tile_home.start()
-
-    ph_sems = (ph_send, ph_recv)
-    ph_along = []
-    for k, p in enumerate(peers):
-        cp = copy_to(
-            pheno.at[pl.ds(rep * half, half), pl.ds(pl.multiple_of(p * n, n), n)],
-            ph_all.at[pl.ds(f * persons + rep * half, half)],
-            ph_sems,
-            k,
-            fam=p,
-        )
-        cp.start()
-        ph_along.append(cp)
 
     keep = [
         pltpu.make_async_copy(imeta, imeta_all.at[me], local_sem.at[0]),
@@ -379,47 +340,46 @@
     to_scalar = pltpu.make_async_copy(inv_v, inv, local_sem.at[4])
     to_scalar.start()
 
-    one_hot_rows(c, col_col, entries, 64)
-    one_hot_cols(ct, col_row, every, 64)
     tile_across, tile_side = [], []
-    for k, s in enumerate(origin):
-        if k == 0:
-            to_near.wait()
-        else:
-            copy_to(own_share, tiles_of(s, rep, t), tile_sems, k, fam=near).wait_recv()
-
-        @pl.when(is_inner)
-        def _():
-            relays[k + 1].start()
-
+    for k, s in enumerate(sources):
+        along[k].wait()
         cp = copy_to(tiles_of(s, rep, t), tiles_of(s, rep, t), tile_sems, k3 + k, trait=across)
         cp.start()
         tile_across.append(cp)
         cp = copy_to(tiles_of(s, rep, t), tiles_of(s, rep, t), tile_sems, 2 * k3 + k, rep=other)
         cp.start()
         tile_side.append(cp)
+    ph_sems = (ph_send, ph_recv)
+    ph_along = []
+    for k, p in enumerate(peers):
+        cp = copy_to(
+            pheno.at[pl.ds(rep * half, half), pl.ds(pl.multiple_of(p * n, n), n)],
+            ph_all.at[pl.ds(f * persons + rep * half, half)],
+            ph_sems,
+            k,
+            fam=p,
+        )
+        cp.start()
+        ph_along.append(cp)
+
     one_hot_rows(rsel, row_col, entries, 64)
     for o in range(owners):
         lane = row_row[:, o * eown : (o + 1) * eown]
         sub = lax.broadcasted_iota(jnp.int32, (persons, eown), 0)
         rselt[o] = jnp.where(lane == sub, 1.0, 0.0).astype(jnp.bfloat16)
-    for k, s in enumerate(origin):
+    for k, s in enumerate(sources):
         tile_across[k].wait()
         part = tiles_of(s, rep, across)
         cp = copy_to(part, part, tile_sems, 3 * k3 + k, rep=other)
         cp.start()
         tile_side.append(cp)
+    one_hot_rows(c, col_col, entries, 64)
+    one_hot_cols(ct, col_row, every, 64)
     one_hot_cols(pm, match_row, every, 64)
     to_scalar.wait()
     tile_home.wait()
     for cp in tile_side:
         cp.wait()
-
-    @pl.when(is_inner)
-    def _():
-        for cp in relays:
-            cp.wait_send()
-
 
     def factor(o, _):
         for a2 in range(nblk // 2):
@@ -469,13 +429,19 @@
     def block(o):
         return pl.ds(pl.multiple_of(o * n, n), n)
 
-    def give(src, dst, k, at):
-        cp = copy_to(src.at[pl.ds(peers[k] * persons + rep * half, half)], dst, out_sems, at, fam=peers[k])
+    early = half // 2
+
+    def rows_of(o, first, count):
+        return pl.ds(pl.multiple_of(o * persons + rep * half + first, early), count)
+
+    def give(src, first, count, dst, k, unit):
+        part = src.at[rows_of(peers[k], first, count)]
+        cp = copy_to(part, dst, out_sems, unit * k3 + k, fam=peers[k])
         cp.start()
         return cp
 
-    def give_direction(step):
-        return [give(d.at[step], got.at[step, :, block(f)], k, step * k3 + k) for k in range(k3)]
+    def give_early(src, which):
+        return [give(src, 0, early, got.at[which, :, block(f)], k, which) for k in range(k3)]
 
     def begin(o, carry):
         rr, dd = carry
@@ -486,8 +452,8 @@
         square = v * v
         return rr + colsum(square), dd + colsum(square * diag[person(o), :])
 
-    rr, dd = lax.fori_loop(0, owners, begin, (zero, zero))
-    given = give_direction(0)
+    rr, dd = lax.fori_loop(0, owners, begin, (zero, zero), unroll=True)
+    given = []
 
     def forward(o, yy):
         g = fold(mm(c[entry(o), :], dcat[...])) * weight[entry(o), :]
@@ -507,16 +473,21 @@
         return diag[person(o), :] * d[step, person(o), :] + back
 
     for step in range(ITERS - 1):
-        yy = lax.fori_loop(0, owners, forward, zero)
+        yy = lax.fori_loop(0, owners, forward, zero, unroll=True)
         alpha = rr / (yy + dd)
-        al[step : step + 1, :] = alpha
+        for o in range(owners):
+            at = slice(o * persons, (o + 1) * persons)
+            move = alpha * d[step, at, :]
+            xs[at, :] = move if step == 0 else xs[at, :] + move
+        if step == ITERS - 2:
+            given += give_early(xs, 0)
 
         def descend(o, acc):
             left = r[person(o), :] - alpha * image(o, step)
             r[person(o), :] = left
             return acc + colsum(left * left)
 
-        nxt = lax.fori_loop(0, owners, descend, zero)
+        nxt = lax.fori_loop(0, owners, descend, zero, unroll=True)
         beta = nxt / rr
         rr = nxt
 
@@ -526,50 +497,49 @@
             dcat[person(o), :] = split_terms(v)
             return acc + colsum(v * v * diag[person(o), :])
 
-        dd = lax.fori_loop(0, owners, turn, zero)
-        given += give_direction(step + 1)
+        dd = lax.fori_loop(0, owners, turn, zero, unroll=True)
 
     last = ITERS - 1
-    yy = lax.fori_loop(0, owners, forward, zero)
+    given += give_early(d.at[last], 1)
+    yy = lax.fori_loop(0, owners, forward, zero, unroll=True)
     alpha = rr / (yy + dd)
-    al[last : last + 1, :] = alpha
-    base = ITERS * k3
-    told = []
+    al[0:1, :] = alpha
     for k in range(k3):
-        cp = copy_to(al, al_all.at[f], out_sems, base + k, fam=peers[k])
-        cp.start()
-        told.append(cp)
+        cp = copy_to(al, al_all.at[f], out_sems, 2 * k3 + k, fam=peers[k])
+        cp.start()
+        given.append(cp)
 
     mine = pl.ds(rep * half, half)
+    mine_early = pl.ds(rep * half, early)
+    mine_late = pl.ds(rep * half + early, half - early)
+    for k in range(k3):
+        at = rows_of(peers[k], early, half - early)
+        xs[at, :] = xs[at, :] + alpha * d[last, at, :]
+        given.append(give(xs, early, half - early, x_out.at[mine_late, block(f)], k, 3))
     theirs = []
     for k in range(owners):
         o = peers[k] if k < k3 else f
         r[person(o), :] = r[person(o), :] - alpha * image(o, last)
         if k < k3:
-            theirs.append(give(r, r_out.at[mine, block(f)], k, base + k3 + k))
+            theirs.append(give(r, 0, half, r_out.at[mine, block(f)], k, 4))
     stay = pltpu.make_async_copy(
         r.at[pl.ds(f * persons, persons)], r_out.at[:, block(f)], local_sem.at[5]
     )
     stay.start()
-    for cp in given + told:
+    for cp in given:
         cp.wait()
 
-    home = pl.ds(f * persons + rep * half, half)
-    total = al[0:1, :] * d[0, home, :]
-    for u in range(1, ITERS):
-        total = total + al[u : u + 1, :] * d[u, home, :]
-    x_out[mine, block(f)] = total
+    home = rows_of(f, 0, half)
+    x_out[mine, block(f)] = xs[home, :] + alpha * d[last, home, :]
     for s in sources:
-        total = al_all[s, 0:1, :] * got[0, :, block(s)]
-        for u in range(1, ITERS):
-            total = total + al_all[s, u : u + 1, :] * got[u, :, block(s)]
-        x_out[mine, block(s)] = total
-    side = [copy_to(x_out.at[mine], x_out.at[mine], out_sems, base + 2 * k3, rep=other)]
+        x_out[mine_early, block(s)] = got[0, :, block(s)] + al_all[s, 0:1, :] * got[1, :, block(s)]
+    base = 5 * k3
+    side = [copy_to(x_out.at[mine], x_out.at[mine], out_sems, base, rep=other)]
     side[0].start()
     for i, cp in enumerate(theirs):
         cp.wait()
         part = r_out.at[mine, block(sources[i])]
-        cp = copy_to(part, part, out_sems, base + 2 * k3 + 1 + i, rep=other)
+        cp = copy_to(part, part, out_sems, base + 1 + i, rep=other)
         cp.start()
         side.append(cp)
     for cp in side + [stay]:
@@ -633,7 +603,8 @@
             pltpu.VMEM((owners, persons, eown), bf),
             pltpu.VMEM((ITERS, every, n), f32),
             pltpu.VMEM((every, n), f32),
-            pltpu.VMEM((ITERS, persons // 2, columns), f32),
+            pltpu.VMEM((every, n), f32),
+            pltpu.VMEM((2, persons // 4, columns), f32),
             pltpu.VMEM((8, n), f32),
             pltpu.VMEM((owners, 8, n), f32),
             pltpu.VMEM((every, 2 * n), bf),
@@ -645,9 +616,8 @@
             dma((4 * k3 + 1,)),
             dma((2 * k3,)),
             dma((2 * k3,)),
-            dma(((ITERS + 3) * k3 + 1,)),
-            dma(((ITERS + 3) * k3 + 1,)),
-            dma((4,)),
+            dma((6 * k3 + 1,)),
+            dma((6 * k3 + 1,)),
             dma((7,)),
         ],
         compiler_params=pltpu.CompilerParams(

time: 93.9 us -> 83.1 us (0.88)
  Pallas kernels: 89.8 us -> 79 us
    pallas_call x1, Pallas kernels: 89.8 us -> 79 us  [local_group(): pl.pallas_call(functools.partial(group_kernel, owners), out_shape=[jax.Sh...]
where the time goes in v4:
time: 83.1 us; the launch traced here: 83 us
  Pallas kernels  79 us (95%)
  local copies, waits for them, and re-layouts  3.32 us (4%)
    pallas_call x1, Pallas kernels, local_group(): pl.pallas_call(functools.partial(group_kernel, owners), out_shape=[jax.Sh...  79 us
    unnamed x4, local copies, waits for them, and re-layouts  3.32 us

profile of v4, /device:TPU:25, one launch (start us, length us, event | category | flops | bytes accessed | tf_op | source)
XLA Modules:
  0.0 83.0 jit_solution(12618452033250158385)
XLA Ops:
  0.6 79.0 %shard_map.113 = (f32[512,512]{1,0:T(8,128)}, f32[512,512]{1,0:T(8,128)}) custom-call(s32[4,128]{1,0:T(4,128)} %bitcast.8, f32[4,128]{1,0:T(4,128)} %bitcast.9, f32[16,4096]{1,0:T(8,128)} %tiles.1, s32[1,16]{1,0:T(1,128)} %bitcast.10, s32[1,16]{1,0:T(1,128)} %bitcast.11, s32[1,128]{1,0:T(1,128)} %bitcast.12, s32[1,128]{1,0:T(1,128)} %bitcast.13, ...), custom_call_target="tpu_custom_call" | custom-call | tf_op jit(solution)/shard_map/pallas_call | solution.py:573
  79.6 0.0 copy-start
  79.6 2.4 %copy.14 = f32[512,512]{1,0:T(8,128)} copy(f32[512,512]{1,0:T(8,128)} %get-tuple-element.4) | data formatting | bytes 2097152
  82.0 0.0 copy-done
  82.0 1.0 %copy.15 = f32[512,512]{1,0:T(8,128)} copy(f32[512,512]{1,0:T(8,128)S(1)} %copy-done) | data formatting | bytes 2097152
Async XLA Ops:
  79.6 2.4 %copy-start = (f32[512,512]{1,0:T(8,128)S(1)}, f32[512,512]{1,0:T(8,128)}, u32[]{:S(2)}) copy-start(f32[512,512]{1,0:T(8,128)} %get-tuple-element.5) | copy-start | bytes 3145732

commit v5 on v4

--- a/solution.py
+++ b/solution.py
@@ -410,10 +410,10 @@
         ph_side.append(cp)
 
     def person(o):
-        return pl.ds(pl.multiple_of(o * persons, persons), persons)
+        return pl.ds(o * persons, persons) if isinstance(o, int) else pl.ds(pl.multiple_of(o * persons, persons), persons)
 
     def entry(o):
-        return pl.ds(pl.multiple_of(o * eown, eown), eown)
+        return pl.ds(o * eown, eown) if isinstance(o, int) else pl.ds(pl.multiple_of(o * eown, eown), eown)
 
     zero = jnp.zeros((1, n), jnp.float32)
 
@@ -455,16 +455,22 @@
     rr, dd = lax.fori_loop(0, owners, begin, (zero, zero), unroll=True)
     given = []
 
-    def forward(o, yy):
-        g = fold(mm(c[entry(o), :], dcat[...])) * weight[entry(o), :]
-        near = dcat[person(o), :]
-        y = fold(mm(khi[o], near) + mm(rselt[o], split_terms(g)))
-        y = y + mm(klo[o], near[:, :n])
-        ys = split_terms(y)
-        ycat[person(o), :] = ys
-        h = fold(mm(rsel[entry(o), :], ys)) * weight[entry(o), :]
-        hcat[entry(o), :] = split_terms(h)
-        return yy + colsum(y * y)
+    def forward():
+        spread = []
+        for o in range(owners):
+            g = fold(mm(c[entry(o), :], dcat[...])) * weight[entry(o), :]
+            spread.append(split_terms(g))
+        yy = zero
+        for o in range(owners):
+            near = dcat[person(o), :]
+            y = fold(mm(khi[o], near) + mm(rselt[o], spread[o]))
+            y = y + mm(klo[o], near[:, :n])
+            ycat[person(o), :] = split_terms(y)
+            yy = yy + colsum(y * y)
+        for o in range(owners):
+            h = fold(mm(rsel[entry(o), :], ycat[person(o), :])) * weight[entry(o), :]
+            hcat[entry(o), :] = split_terms(h)
+        return yy
 
     def image(o, step):
         ys = ycat[person(o), :]
@@ -473,7 +479,7 @@
         return diag[person(o), :] * d[step, person(o), :] + back
 
     for step in range(ITERS - 1):
-        yy = lax.fori_loop(0, owners, forward, zero, unroll=True)
+        yy = forward()
         alpha = rr / (yy + dd)
         for o in range(owners):
             at = slice(o * persons, (o + 1) * persons)
@@ -501,7 +507,7 @@
 
     last = ITERS - 1
     given += give_early(d.at[last], 1)
-    yy = lax.fori_loop(0, owners, forward, zero, unroll=True)
+    yy = forward()
     alpha = rr / (yy + dd)
     al[0:1, :] = alpha
     for k in range(k3):

time: 83.1 us -> 81.4 us (0.980)
  Pallas kernels: 79 us -> 77.2 us
    pallas_call x1, Pallas kernels: 79 us -> 77.2 us  [local_group(): pl.pallas_call(functools.partial(group_kernel, owners), out_shape=[jax.Sh...]
where the time goes in v5:
time: 81.4 us; the launch traced here: 81.2 us
  Pallas kernels  77.2 us (95%)
  local copies, waits for them, and re-layouts  3.32 us (4%)
    pallas_call x1, Pallas kernels, local_group(): pl.pallas_call(functools.partial(group_kernel, owners), out_shape=[jax.Sh...  77.2 us
    unnamed x4, local copies, waits for them, and re-layouts  3.32 us

profile of v5, /device:TPU:25, one launch (start us, length us, event | category | flops | bytes accessed | tf_op | source)
XLA Modules:
  0.0 81.2 jit_solution(2746810164785321028)
XLA Ops:
  0.6 77.2 %shard_map.113 = (f32[512,512]{1,0:T(8,128)}, f32[512,512]{1,0:T(8,128)}) custom-call(s32[4,128]{1,0:T(4,128)} %bitcast.8, f32[4,128]{1,0:T(4,128)} %bitcast.9, f32[16,4096]{1,0:T(8,128)} %tiles.1, s32[1,16]{1,0:T(1,128)} %bitcast.10, s32[1,16]{1,0:T(1,128)} %bitcast.11, s32[1,128]{1,0:T(1,128)} %bitcast.12, s32[1,128]{1,0:T(1,128)} %bitcast.13, ...), custom_call_target="tpu_custom_call" | custom-call | tf_op jit(solution)/shard_map/pallas_call | solution.py:579
  77.9 0.0 copy-start
  77.9 2.4 %copy.14 = f32[512,512]{1,0:T(8,128)} copy(f32[512,512]{1,0:T(8,128)} %get-tuple-element.4) | data formatting | bytes 2097152
  80.2 0.0 copy-done
  80.2 1.0 %copy.15 = f32[512,512]{1,0:T(8,128)} copy(f32[512,512]{1,0:T(8,128)S(1)} %copy-done) | data formatting | bytes 2097152
Async XLA Ops:
  77.9 2.4 %copy-start = (f32[512,512]{1,0:T(8,128)S(1)}, f32[512,512]{1,0:T(8,128)}, u32[]{:S(2)}) copy-start(f32[512,512]{1,0:T(8,128)} %get-tuple-element.5) | copy-start | bytes 3145732
